TPU v7x, 256 devices: a whole 4x4x8 slice. The times are simulated.
256 devices in a mesh: dp: 4 (over y), expert: 64 (over x, z, core).
Axes of the slice: x: 4, y: 4, z: 8, core: 2. Of those that a mesh axis runs over, the one named last changes fastest.
Arguments:
- tokens: bfloat16 [8192, 3584], P('expert', 'dp'), may hold values from -6 to 6
- grad_out: bfloat16 [8192, 3584], P('expert', 'dp'), may hold values from -1.5 to 1.5
- routes: int32 [8192, 2], P('expert'), may hold values from 0 to 63, all different within a row; in each aligned block of 128 rows (0 to 127, 128 to 255, ...) at most 8 rows name the same one
- gates: bfloat16 [8192, 2], P('expert'), may hold values from 0.19921875 to 1
- replicated: int32 [64], P('expert'), may hold values from 0 to 1, as said below
- w_gate: bfloat16 [64, 3584, 1024], P('expert', None, 'dp'), as said below
- w_up: bfloat16 [64, 3584, 1024], P('expert', None, 'dp'), as said below
- w_down: bfloat16 [64, 1024, 3584], P('expert', 'dp'), as said below
Outputs:
- grad_tokens: bfloat16 [8192, 3584], P('expert', 'dp')
- grad_gate: bfloat16 [64, 3584, 1024], P('expert', None, 'dp')
- grad_up: bfloat16 [64, 3584, 1024], P('expert', None, 'dp')
- grad_down: bfloat16 [64, 1024, 3584], P('expert', 'dp')
Inputs may be any that keep to these rules, and one draw needn't show every extreme that they name: `routes`: A token names 2 different slots. Among the entries of the tokens of one index of expert (aligned blocks of 128 rows) no slot is named more than 8 times, a bound that some block reaches. `replicated`: equal in the two slots 2j and 2j + 1 of a pair; one to all but one of the 32 pairs hold 1. `w_gate`: the two slots of a pair with replicated 1 hold equal weights. `w_up`: the two slots of a pair with replicated 1 hold equal weights. `w_down`: the two slots of a pair with replicated 1 hold equal weights.
All inputs are finite; a program needn't handle non-finite values.
Results may differ from a plain program's by a relative error of at most 0.0054.
Values may be sent and summed in bfloat16 or wider, within the bound.
A program may use at most 128 MiB of HBM per device.

v0:
```python
import jax
import jax.numpy as jnp
from jax import lax
from jax.sharding import PartitionSpec as P


def from_partner(value, axis, bit):
    return lax.ppermute(value, axis, [(i, i ^ 1 << bit) for i in range(lax.axis_size(axis))])


def expert_backward(x_rows, dy_rows, gate_col, weight_gate, weight_up, weight_down):
    pre_gate = jnp.dot(x_rows, weight_gate, preferred_element_type=jnp.float32)
    pre_up = jnp.dot(x_rows, weight_up, preferred_element_type=jnp.float32)
    sigmoid_v = jax.nn.sigmoid(pre_gate)
    activated = pre_gate * sigmoid_v
    scaled_hidden = (gate_col * activated * pre_up).astype(jnp.bfloat16)
    d_hidden = gate_col * lax.dot_general(
        dy_rows, weight_down, (((1,), (1,)), ((), ())), preferred_element_type=jnp.float32
    )
    d_up = (d_hidden * activated).astype(jnp.bfloat16)
    d_gate = (d_hidden * pre_up * sigmoid_v * (1.0 + pre_gate * (1.0 - sigmoid_v))).astype(
        jnp.bfloat16
    )
    grad_gate = lax.dot_general(
        x_rows, d_gate, (((0,), (0,)), ((), ())), preferred_element_type=jnp.float32
    )
    grad_up = lax.dot_general(
        x_rows, d_up, (((0,), (0,)), ((), ())), preferred_element_type=jnp.float32
    )
    grad_down = lax.dot_general(
        scaled_hidden, dy_rows, (((0,), (0,)), ((), ())), preferred_element_type=jnp.float32
    )
    d_rows = lax.dot_general(
        d_gate, weight_gate, (((1,), (1,)), ((), ())), preferred_element_type=jnp.float32
    )
    d_rows = d_rows + lax.dot_general(
        d_up, weight_up, (((1,), (1,)), ((), ())), preferred_element_type=jnp.float32
    )
    return (d_rows, grad_gate, grad_up, grad_down)


def on_device(tokens, grad_out, routes, gates, replicated, w_gate, w_up, w_down):
    row_count = tokens.shape[0]
    top_count = routes.shape[1]
    slot_count = lax.axis_size("expert")
    capacity = 2 * row_count * top_count // slot_count
    buffer_rows = slot_count * capacity
    flat_routes = routes.reshape(-1)
    one_hot = (flat_routes[:, None] == jnp.arange(slot_count, dtype=jnp.int32)[None, :]).astype(
        jnp.int32
    )
    earlier = jnp.cumsum(one_hot, axis=0) - one_hot
    slot_rank = jnp.sum(earlier * one_hot, axis=1)
    target = flat_routes * capacity + slot_rank
    source_row = jnp.arange(row_count * top_count, dtype=jnp.int32) // top_count
    gate_buffer = jnp.zeros((buffer_rows,), gates.dtype).at[target].set(gates.reshape(-1))

    def packed(matrix):
        return (
            jnp.zeros((buffer_rows, matrix.shape[1]), matrix.dtype)
            .at[target]
            .set(matrix[source_row])
        )

    full_x, full_dy = (
        lax.all_gather(tokens, "dp", axis=1, tiled=True),
        lax.all_gather(grad_out, "dp", axis=1, tiled=True),
    )
    x_rows, dy_rows, gate_rows = (
        lax.all_to_all(packed(full_x), "expert", split_axis=0, concat_axis=0, tiled=True),
        lax.all_to_all(packed(full_dy), "expert", split_axis=0, concat_axis=0, tiled=True),
        lax.all_to_all(gate_buffer, "expert", split_axis=0, concat_axis=0, tiled=True),
    )
    gate_col = gate_rows.astype(jnp.float32)[:, None]
    d_rows, grad_gate, grad_up, grad_down = expert_backward(
        x_rows, dy_rows, gate_col, w_gate[0], w_up[0], w_down[0]
    )
    own_grads = (
        grad_gate.astype(jnp.bfloat16),
        grad_up.astype(jnp.bfloat16),
        grad_down.astype(jnp.bfloat16),
    )
    partner_grads = from_partner((own_grads[0], own_grads[1], own_grads[2]), "expert", 0)
    replica_flag = replicated[0] == 1
    merged = []
    for mine, theirs in zip(own_grads, partner_grads):
        added = (mine.astype(jnp.float32) + theirs.astype(jnp.float32)).astype(jnp.bfloat16)
        merged.append(jnp.where(replica_flag, added, mine)[None])
    reduced = lax.psum_scatter(d_rows, "dp", scatter_dimension=1, tiled=True)
    returned = lax.all_to_all(reduced, "expert", split_axis=0, concat_axis=0, tiled=True)
    grad_tokens = (
        returned[target].reshape(row_count, top_count, -1).sum(axis=1).astype(jnp.bfloat16)
    )
    return (grad_tokens, merged[0], merged[1], merged[2])


def solution(mesh):
    return jax.shard_map(
        on_device,
        mesh=mesh,
        in_specs=(
            P("expert", "dp"),
            P("expert", "dp"),
            P("expert", None),
            P("expert", None),
            P("expert"),
            P("expert", None, "dp"),
            P("expert", None, "dp"),
            P("expert", "dp", None),
        ),
        out_specs=(
            P("expert", "dp"),
            P("expert", None, "dp"),
            P("expert", None, "dp"),
            P("expert", "dp", None),
        ),
        check_vma=False,
    )
```

profile of v0, /device:TPU:1, one launch (start us, length us, event | category | flops | bytes accessed | tf_op | source)
XLA Modules:
  0.0 391.6 jit_solution(2256372786783487246)
XLA Ops:
  7.2 0.9 copy.18
  8.4 0.7 broadcast_multiply_fusion
  10.2 0.8 copy.21
  11.2 2.2 scatter_custom_fusion
  13.4 0.7 all_to_all.41
  14.1 13.0 %all-to-all-start = ((bf16[64,8,1]{1,2,0:T(2,128)(2,1)}), bf16[64,8,1]{1,2,0:T(2,128)(2,1)S(1)}, u32[]{:S(2)}, u32[]{:S(2)}) async-start(bf16[64,8,1]{1,2,0:T(2,128)(2,1)} %all_to_all.41), calls=%async_computation | async-start | bytes 65536 | tf_op jit(solution)/shard_map/all_to_all | solution.py:72
  27.1 13.7 %all_gather.7 = bf16[128,3584]{1,0:T(8,128)(2,1)S(1)} all-gather(bf16[128,896]{1,0:T(8,128)(2,1)} %param.8), channel_id=1, replica_groups=mesh['dp'=4,'expert'=64] {'dp'}, dimensions={1}, use_global_device_ids=true | all-gather | bytes 1146880 | tf_op jit(solution)/shard_map/all_gather | solution.py:66
  40.8 10.9 %scatter_custom_fusion.2 = bf16[512,3584]{1,0:T(8,128)(2,1)} fusion(s32[256]{0:T(256)S(1)} %bitcast.77, bf16[128,3584]{1,0:T(8,128)(2,1)S(1)} %all_gather.7, s32[1024]{0:T(1024)S(1)} %pad_clamp_fusion.1, bf16[]{:T(256)} %constant.28.clone.1), kind=kCustom, calls=%fused_computation.34 | custom fusion | bytes 3670018 | tf_op jit(solution)/shard_map/scatter | solution.py:62
  51.7 12.7 %all-to-all-start.2 = ((bf16[64,8,3584]{2,1,0:T(8,128)(2,1)}), bf16[64,8,3584]{2,1,0:T(8,128)(2,1)}, u32[]{:S(2)}, u32[]{:S(2)}) async-start(bf16[64,8,3584]{2,1,0:T(8,128)(2,1)} %bitcast.73), calls=%async_computation.2 | async-start | bytes 7340032 | tf_op jit(solution)/shard_map/all_to_all | solution.py:70
  64.4 13.7 %all_gather.6 = bf16[128,3584]{1,0:T(8,128)(2,1)S(1)} all-gather(bf16[128,896]{1,0:T(8,128)(2,1)S(1)} %copy-done.3), channel_id=1, replica_groups=mesh['dp'=4,'expert'=64] {'dp'}, dimensions={1}, use_global_device_ids=true | all-gather | bytes 1146880 | tf_op jit(solution)/shard_map/all_gather | solution.py:67
  78.2 11.0 %scatter_custom_fusion.1 = bf16[512,3584]{1,0:T(8,128)(2,1)} fusion(s32[256]{0:T(256)S(1)} %bitcast.78, bf16[128,3584]{1,0:T(8,128)(2,1)S(1)} %all_gather.6, s32[1024]{0:T(1024)S(1)} %pad_clamp_fusion.1, bf16[]{:T(256)} %constant.28.clone.1), kind=kCustom, calls=%fused_computation.36 | custom fusion | bytes 3670018 | tf_op jit(solution)/shard_map/scatter | solution.py:62
  89.1 60.0 %all-to-all-done.2 = bf16[64,8,3584]{2,1,0:T(8,128)(2,1)} async-done(((bf16[64,8,3584]{2,1,0:T(8,128)(2,1)}), bf16[64,8,3584]{2,1,0:T(8,128)(2,1)}, u32[]{:S(2)}, u32[]{:S(2)}) %all-to-all-start.2) | async-done | bytes 3670048 | tf_op jit(solution)/shard_map/all_to_all | solution.py:70
  149.1 5.9 %all-to-all-start.1 = ((bf16[64,8,3584]{2,1,0:T(8,128)(2,1)}), bf16[64,8,3584]{2,1,0:T(8,128)(2,1)}, u32[]{:S(2)}, u32[]{:S(2)}) async-start(bf16[64,8,3584]{2,1,0:T(8,128)(2,1)} %bitcast.72), calls=%async_computation.1 | async-start | bytes 7340032 | tf_op jit(solution)/shard_map/all_to_all | solution.py:71
  155.5 3.3 fusion.2
  158.8 3.1 fusion.4
  161.9 77.7 %all-to-all-done.1 = bf16[64,8,3584]{2,1,0:T(8,128)(2,1)} async-done(((bf16[64,8,3584]{2,1,0:T(8,128)(2,1)}), bf16[64,8,3584]{2,1,0:T(8,128)(2,1)}, u32[]{:S(2)}, u32[]{:S(2)}) %all-to-all-start.1) | async-done | bytes 3670048 | tf_op jit(solution)/shard_map/all_to_all | solution.py:71
  239.7 3.8 multiply_convert_fusion.1
  243.5 1.2 fusion.15
  245.0 4.2 %convolution_add_fusion = f32[512,3584]{1,0:T(8,128)} fusion(f32[512,3584]{1,0:T(8,128)S(1)} %fusion.15, bf16[512,256]{1,0:T(8,128)(2,1)S(1)} %get-tuple-element.4, bf16[1,3584,256]{2,1,0:T(8,128)(2,1)S(1)} %copy-done.2), kind=kOutput, calls=%fused_computation.6 | convolution fusion | flops 941359104 | bytes 16777216 | tf_op jit(solution)/shard_map/dot_general | solution.py:36
  249.2 4.5 %convolution_convert_fusion = bf16[256,3584]{1,0:T(8,128)(2,1)} fusion(bf16[64,8,3584]{2,1,0:T(8,128)(2,1)} %all-to-all-done.1, f32[512,256]{1,0:T(8,128)S(1)} %fusion.4, f32[512]{0:T(512)S(1)} %reshape.123, f32[512,256]{1,0:T(8,128)S(1)} %fusion.2), kind=kOutput, calls=%fused_computation.7 | convolution fusion | flops 941359104 | bytes 6555648 | tf_op jit(solution)/shard_map/dot_general | solution.py:30
  254.1 4.4 %convolution_convert_fusion.1 = bf16[3584,256]{1,0:T(8,128)(2,1)} fusion(bf16[512,256]{1,0:T(8,128)(2,1)S(1)} %get-tuple-element.4, bf16[64,8,3584]{2,1,0:T(8,128)(2,1)} %all-to-all-done.2), kind=kOutput, calls=%fused_computation.8 | convolution fusion | flops 940441600 | bytes 5767168 | tf_op jit(solution)/shard_map/dot_general | solution.py:27
  258.7 62.2 %reduce-scatter.2.cloned.1.call-done = f32[512,896]{1,0:T(8,128)} async-done(((f32[512,3584]{1,0:T(8,128)}), f32[512,896]{1,0:T(8,128)}) %reduce-scatter.2.cloned.1.call-update) | async-done | bytes 1835024 | tf_op jit(solution)/shard_map/reduce_scatter | solution.py:89
  320.9 10.8 %all-to-all-start.3 = ((f32[64,8,896]{2,1,0:T(8,128)}), f32[64,8,896]{2,1,0:T(8,128)}, u32[]{:S(2)}, u32[]{:S(2)}) async-start(f32[64,8,896]{2,1,0:T(8,128)} %bitcast.74), calls=%async_computation.4 | async-start | bytes 3670016 | tf_op jit(solution)/shard_map/all_to_all | solution.py:90
  332.4 3.2 convolution_convert_fusion.2
  335.6 0.9 collective-permute-start
  336.5 4.5 %fusion.12 = bf16[1,256,3584]{2,1,0:T(8,128)(2,1)} fusion(bf16[256,3584]{1,0:T(8,128)(2,1)} %convolution_convert_fusion, bf16[256,3584]{1,0:T(8,128)(2,1)} %collective-permute-done.2, pred[]{:T(512)} %bitcast.13), kind=kLoop, calls=%fused_computation.25 | loop fusion | flops 4587520 | bytes 5505025 | tf_op jit(solution)/shard_map/broadcast_in_dim | solution.py:88
  340.9 4.5 %fusion.13 = bf16[1,3584,256]{2,1,0:T(8,128)(2,1)} fusion(bf16[3584,256]{1,0:T(8,128)(2,1)} %convolution_convert_fusion.1, bf16[3584,256]{1,0:T(8,128)(2,1)} %collective-permute-done.1, pred[]{:T(512)} %bitcast.13), kind=kLoop, calls=%fused_computation.26 | loop fusion | flops 4587520 | bytes 5505025 | tf_op jit(solution)/shard_map/broadcast_in_dim | solution.py:88
  345.4 1.8 fusion.14
  347.3 29.8 %all-to-all-done.3 = f32[64,8,896]{2,1,0:T(8,128)} async-done(((f32[64,8,896]{2,1,0:T(8,128)}), f32[64,8,896]{2,1,0:T(8,128)}, u32[]{:S(2)}, u32[]{:S(2)}) %all-to-all-start.3) | async-done | bytes 1835040 | tf_op jit(solution)/shard_map/all_to_all | solution.py:90
  377.1 3.0 gather_fusion
  380.1 1.5 reshape.122
  381.5 3.0 reduce_sum.22
  (33 shorter events, 3.0 us)
Async XLA Ops:
  7.2 148.3 %copy-start = (bf16[1,3584,256]{2,1,0:T(8,128)(2,1)S(1)}, bf16[1,3584,256]{2,1,0:T(8,128)(2,1)}, u32[]{:S(2)}) copy-start(bf16[1,3584,256]{2,1,0:T(8,128)(2,1)} %param.13) | copy-start | bytes 5505028
  14.1 37.6 %all-to-all-start = ((bf16[64,8,1]{1,2,0:T(2,128)(2,1)}), bf16[64,8,1]{1,2,0:T(2,128)(2,1)S(1)}, u32[]{:S(2)}, u32[]{:S(2)}) async-start(bf16[64,8,1]{1,2,0:T(2,128)(2,1)} %all_to_all.41), calls=%async_computation | async-start | bytes 65536 | tf_op jit(solution)/shard_map/all_to_all | solution.py:72
  51.7 12.7 %copy-start.3 = (bf16[128,896]{1,0:T(8,128)(2,1)S(1)}, bf16[128,896]{1,0:T(8,128)(2,1)}, u32[]{:S(2)}) copy-start(bf16[128,896]{1,0:T(8,128)(2,1)} %param.9) | copy-start | bytes 688132
  51.7 97.4 %all-to-all-start.2 = ((bf16[64,8,3584]{2,1,0:T(8,128)(2,1)}), bf16[64,8,3584]{2,1,0:T(8,128)(2,1)}, u32[]{:S(2)}, u32[]{:S(2)}) async-start(bf16[64,8,3584]{2,1,0:T(8,128)(2,1)} %bitcast.73), calls=%async_computation.2 | async-start | bytes 7340032 | tf_op jit(solution)/shard_map/all_to_all | solution.py:70
  149.1 90.6 %all-to-all-start.1 = ((bf16[64,8,3584]{2,1,0:T(8,128)(2,1)}), bf16[64,8,3584]{2,1,0:T(8,128)(2,1)}, u32[]{:S(2)}, u32[]{:S(2)}) async-start(bf16[64,8,3584]{2,1,0:T(8,128)(2,1)} %bitcast.72), calls=%async_computation.1 | async-start | bytes 7340032 | tf_op jit(solution)/shard_map/all_to_all | solution.py:71
  155.0 165.9 %reduce-scatter.2.cloned.1.call-start = ((), (), s32[]{:S(2)}) async-start(), calls=%async_computation.5 | async-start | bytes 9175040 | tf_op jit(solution)/shard_map/reduce_scatter | solution.py:89
  155.5 3.3 copy-start.1
  243.5 1.5 copy-start.2
  253.8 82.7 %collective-permute-start.2 = (bf16[256,3584]{1,0:T(8,128)(2,1)}, bf16[256,3584]{1,0:T(8,128)(2,1)}, u32[]{:S(2)}, u32[]{:S(2)}) collective-permute-start(bf16[256,3584]{1,0:T(8,128)(2,1)} %convolution_convert_fusion), channel_id=1, source_target_pairs={{0,1},{1,0},{2,3},{3,2},{4,5},{5,4},{6,7},{7,6},{8,9},{9,8},{10,11... | collective-permute-start | bytes 5505032 | tf_op jit(solution)/shard_map/ppermute | solution.py:8
  258.6 82.4 %collective-permute-start.1 = (bf16[3584,256]{1,0:T(8,128)(2,1)}, bf16[3584,256]{1,0:T(8,128)(2,1)}, u32[]{:S(2)}, u32[]{:S(2)}) collective-permute-start(bf16[3584,256]{1,0:T(8,128)(2,1)} %convolution_convert_fusion.1), channel_id=1, source_target_pairs={{0,1},{1,0},{2,3},{3,2},{4,5},{5,4},{6,7},{7,6},{8,9},{9,8},{10,11... | collective-permute-start | bytes 5505032 | tf_op jit(solution)/shard_map/ppermute | solution.py:8
  320.9 56.1 %all-to-all-start.3 = ((f32[64,8,896]{2,1,0:T(8,128)}), f32[64,8,896]{2,1,0:T(8,128)}, u32[]{:S(2)}, u32[]{:S(2)}) async-start(f32[64,8,896]{2,1,0:T(8,128)} %bitcast.74), calls=%async_computation.4 | async-start | bytes 3670016 | tf_op jit(solution)/shard_map/all_to_all | solution.py:90
  335.6 9.8 %collective-permute-start = (bf16[3584,256]{1,0:T(8,128)(2,1)S(1)}, bf16[3584,256]{1,0:T(8,128)(2,1)S(1)}, u32[]{:S(2)}, u32[]{:S(2)}) collective-permute-start(bf16[3584,256]{1,0:T(8,128)(2,1)S(1)} %convolution_convert_fusion.2), channel_id=1, source_target_pairs={{0,1},{1,0},{2,3},{3,2},{4,5},{5,4},{6,7},{7,6},{8,9},{9,8},{10,11... | collective-permute-start | bytes 5505032 | tf_op jit(solution)/shard_map/ppermute | solution.py:8
Sparse Core Ops, SparseCore 0:
  249.4 71.5 reduce-scatter.1
where the time goes:
time: 396 us; the launch traced here: 392 us
  waiting for transfers between devices  230 us (58%)
  starting transfers between devices  44 us (11%)
  local copies, waits for them, and re-layouts  32.2 us (8%)
  matrix products  27.8 us (7%)
  blocking collectives  27.4 us (7%)
  other arithmetic  15.3 us (4%)
  between operations  15.1 us (4%)
    all_to_all x1, waiting for transfers between devices, on_device(): lax.all_to_all(packed(full_dy), 'expert', split_axis=0, concat_axis=0, ti...  77.7 us
    reduce_scatter x1, waiting for transfers between devices, on_device(): reduced = lax.psum_scatter(d_rows, 'dp', scatter_dimension=1, tiled=True)  62.2 us
    all_to_all x1, waiting for transfers between devices, on_device(): lax.all_to_all(packed(full_x), 'expert', split_axis=0, concat_axis=0, til...  60 us
    all_to_all x1, waiting for transfers between devices, on_device(): lax.all_to_all(reduced, 'expert', split_axis=0, concat_axis=0, tiled=True)  29.8 us
    scatter x2, local copies, waits for them, and re-layouts, packed(): return jnp.zeros((buffer_rows, matrix.shape[1]), matrix.dtype).at[target]...  21.8 us
    all_gather x1, blocking collectives, on_device(): lax.all_gather(grad_out, 'dp', axis=1, tiled=True)  13.7 us
    all_gather x1, blocking collectives, on_device(): lax.all_gather(tokens, 'dp', axis=1, tiled=True)  13.7 us
    all_to_all x1, starting transfers between devices, on_device(): lax.all_to_all(gate_buffer, 'expert', split_axis=0, concat_axis=0, tiled=...  13 us
  transfers between devices with their start and end apart: 8, of which 4 were waited for; matrix products, arithmetic and copies ran while one was open for 13% of the time, Pallas kernels for 0%

commit v1 on v0

v1 whole, which is shorter than its diff:
```python
import functools

import jax
import jax.numpy as jnp
from jax import lax
from jax.experimental import pallas as pl
from jax.experimental.pallas import tpu as pltpu
from jax.sharding import PartitionSpec as P

MESH = pl.DeviceIdType.MESH
BF, F32 = jnp.bfloat16, jnp.float32
D, H, DP = 3584, 1024, 4
FQ, HQ = D // DP, H // DP
TOK, CAP, SLOTS = 128, 8, 64
NX, NZ = 4, 8
NCH = 8
NPAIR = 4
MSG = FQ + 128
RET = 512


def z_step(j):
    return ((j + 1) // 2) * (1 if j % 2 else -1)


OFFSETS = [(dx, z_step(j) % NZ, dc) for dx in (0, 1, 3, 2) for j in range(NZ) for dc in (0, 1)]
BACK = [OFFSETS.index(((-dx) % NX, (-dz) % NZ, dc)) for dx, dz, dc in OFFSETS]


def dot(a, b, dims):
    return lax.dot_general(a, b, ((dims[0], dims[1]), ((), ())), preferred_element_type=F32)


NN, NT, TN = ((1,), (0,)), ((1,), (1,)), ((0,), (0,))


def kernel(
    tok_ref, dy_ref, routes_ref, gates_ref, flag_ref, wg_ref, wu_ref, wd_ref,
    ret_ref, sel_ref, og_ref, ou_ref, od_ref,
    wgu, wdn, sel, msg, land, rows, gcol, dgu, sh,
    rs_snd, rs_a, rs_b, p_up, p_dn, p_own, fin_snd, fin_rcv, rt_snd, rt_rcv,
    gu_mine, gd_mine, gu_theirs, gd_theirs,
    w_sem, loc_sem, a_snd, a_rcv, y_snd, y_rcv, r_snd, r_rcv, q_snd, q_rcv, f_snd, f_rcv,
    b_snd, b_rcv, g_snd, g_rcv, o_sem,
):
    d = lax.axis_index("dp")
    e = lax.axis_index("expert")
    x0, z0, c0 = e // 16, (e // 2) % NZ, e % 2
    up, dn, op = (d + 1) % DP, (d + 3) % DP, (d + 2) % DP

    def peer(o):
        dx, dz, dc = OFFSETS[o]
        return ((x0 + dx) % NX * NZ + (z0 + dz) % NZ) * 2 + (c0 + dc) % 2

    def remote(src, dst, s, r, dev):
        return pltpu.make_async_remote_copy(src, dst, s, r, device_id=dev, device_id_type=MESH)

    weights_in = [
        pltpu.make_async_copy(wg_ref.at[0], wgu.at[:, pl.ds(0, HQ)], w_sem.at[0]),
        pltpu.make_async_copy(wu_ref.at[0], wgu.at[:, pl.ds(HQ, HQ)], w_sem.at[1]),
        pltpu.make_async_copy(wd_ref.at[0], wdn, w_sem.at[2]),
    ]
    for c in weights_in:
        c.start()

    barrier = pltpu.get_barrier_semaphore()
    for o in range(1, SLOTS):
        pl.semaphore_signal(barrier, inc=1, device_id=(d, peer(o)), device_id_type=MESH)
    for q in range(1, DP):
        pl.semaphore_signal(barrier, inc=1, device_id=((d + q) % DP, e), device_id_type=MESH)

    io = lax.broadcasted_iota(jnp.int32, (SLOTS, TOK), 0)
    dxi = io >> 4
    j = (io >> 1) & 7
    mag = (j + 1) >> 1
    slot_x = (x0 + (dxi ^ (dxi >> 1))) & (NX - 1)
    slot_z = (z0 + jnp.where((j & 1) == 1, mag, -mag)) & (NZ - 1)
    slot = (slot_x * NZ + slot_z) * 2 + (c0 ^ (io & 1))
    on0 = routes_ref[0:1, :] == slot
    on1 = routes_ref[1:2, :] == slot
    hot0 = on0.astype(F32)
    hot1 = on1.astype(F32)
    before = (
        lax.broadcasted_iota(jnp.int32, (TOK, TOK), 0) < lax.broadcasted_iota(jnp.int32, (TOK, TOK), 1)
    ).astype(BF)
    rank0 = dot(hot0.astype(BF), before, NN)
    rank1 = dot(hot1.astype(BF), before, NN) + jnp.sum(hot0, axis=1, keepdims=True)
    rank0 = jnp.where(on0, rank0, -1.0).astype(BF)
    rank1 = jnp.where(on1, rank1, -1.0).astype(BF)
    n_rows = SLOTS * CAP
    ui = lax.broadcasted_iota(jnp.int32, (n_rows, SLOTS), 0)
    spread = ((ui >> 3) == lax.broadcasted_iota(jnp.int32, (n_rows, SLOTS), 1)).astype(BF)
    place = (lax.broadcasted_iota(jnp.int32, (n_rows, TOK), 0) & 7).astype(F32)
    sel0 = (dot(spread, rank0, NN) == place).astype(F32)
    sel1 = (dot(spread, rank1, NN) == place).astype(F32)
    sel[...] = (sel0 + sel1).astype(BF)
    gate_of = (sel0 * gates_ref[0:1, :] + sel1 * gates_ref[1:2, :]).astype(BF)
    gcol[...] = dot(gate_of, jnp.ones((TOK, 128), BF), NN)

    a2a = {}
    for k in range(NCH):
        s = sel[k * 64:(k + 1) * 64, :]
        xk = dot(s, tok_ref[...], NN).reshape(8, 8, FQ)
        yk = dot(s, dy_ref[...], NN).reshape(8, 8, FQ)
        gk = gcol[k * 64:(k + 1) * 64, :].reshape(8, 8, 128)
        msg[k * 8:(k + 1) * 8, :, 0:FQ] = jnp.concatenate([xk, yk], axis=1).astype(BF)
        msg[k * 8:(k + 1) * 8, :, FQ:MSG] = jnp.concatenate([gk, gk], axis=1).astype(BF)
        if k == 0:
            pl.semaphore_wait(barrier, SLOTS - 1 + DP - 1)
            own = pltpu.make_async_copy(msg.at[0], land.at[0], loc_sem.at[0])
            own.start()
        for o in range(max(1, 8 * k), 8 * k + 8):
            a2a[o] = remote(msg.at[o], land.at[o], a_snd.at[k], a_rcv.at[k], (d, peer(o)))
            a2a[o].start()

    def chunk_wait(buf, k, sem, per=8):
        lo = max(1, per * k)
        block = buf.at[pl.ds(lo, per * k + per - lo)]
        pltpu.make_async_copy(block, block, sem.at[k]).wait()

    to_up, to_dn, rel_up, rel_dn = {}, {}, {}, {}

    def forward(k):
        if k == 0:
            own.wait()
        chunk_wait(land, k, a_rcv)
        block = land[k * 8:(k + 1) * 8].astype(F32)
        rows[k, d, 0:64, :] = block[:, 0:8, 0:FQ].reshape(64, FQ).astype(BF)
        rows[k, d, 64:128, :] = block[:, 8:16, 0:FQ].reshape(64, FQ).astype(BF)
        gcol[k * 64:(k + 1) * 64, :] = block[:, 0:8, FQ:MSG].reshape(64, 128)
        mine = rows.at[k, d]
        to_up[k] = remote(mine, mine, y_snd.at[k, 0], y_rcv.at[k, 0], (up, e))
        to_dn[k] = remote(mine, mine, y_snd.at[k, 1], y_rcv.at[k, 1], (dn, e))
        to_up[k].start()
        to_dn[k].start()

    def relay(k):
        to_up[k].wait_recv()
        part = rows.at[k, dn, pl.ds(0, 64)]
        rel_up[k] = remote(part, part, r_snd.at[k, 0], r_rcv.at[k, 0], (up, e))
        rel_up[k].start()
        to_dn[k].wait_recv()
        part = rows.at[k, up, pl.ds(64, 64)]
        rel_dn[k] = remote(part, part, r_snd.at[k, 1], r_rcv.at[k, 1], (dn, e))
        rel_dn[k].start()

    def row_part(p, q):
        rng = pl.ds(pl.multiple_of(q * FQ, FQ), FQ)
        return dot(dgu[p * 128:(p + 1) * 128, :], wgu[rng, :], NT)

    rs_c = {}

    def compute(p):
        for k in (2 * p, 2 * p + 1):
            rel_up[k].wait_recv()
            rel_dn[k].wait_recv()
        pre = jnp.zeros((128, 2 * HQ), F32)
        dh = jnp.zeros((128, HQ), F32)
        for q in range(DP):
            xq = rows[2 * p:2 * p + 2, q, 0:64, :].reshape(128, FQ)
            yq = rows[2 * p:2 * p + 2, q, 64:128, :].reshape(128, FQ)
            pre = pre + dot(xq, wgu[q * FQ:(q + 1) * FQ, :], NN)
            dh = dh + dot(yq, wdn[:, q * FQ:(q + 1) * FQ], NT)
        g = gcol[p * 128:(p + 1) * 128, :]
        g = jnp.concatenate([g, g], axis=1)
        pg, pu = pre[:, 0:HQ], pre[:, HQ:]
        sig = jax.nn.sigmoid(pg)
        act = pg * sig
        dh = g * dh
        span = slice(p * 128, (p + 1) * 128)
        sh[span, :] = (g * act * pu).astype(BF)
        dgu[span, 0:HQ] = (dh * pu * sig * (1.0 + pg * (1.0 - sig))).astype(BF)
        dgu[span, HQ:] = (dh * act).astype(BF)
        rs_snd[p] = row_part(p, op).astype(BF)
        rs_c[p] = (
            remote(rs_snd.at[p, pl.ds(0, 64)], rs_a.at[p], q_snd.at[p, 0], q_rcv.at[p, 0], (up, e)),
            remote(rs_snd.at[p, pl.ds(64, 64)], rs_b.at[p], q_snd.at[p, 1], q_rcv.at[p, 1], (dn, e)),
        )
        for c in rs_c[p]:
            c.start()
        p_up[p] = row_part(p, up)
        p_dn[p] = row_part(p, dn)
        p_own[p] = row_part(p, d)

    fin_c = {}

    def stage2(p):
        rs_c[p][0].wait_recv()
        fin_snd[p, 0, 0:64, :] = (p_up[p, 0:64, :] + rs_a[p].astype(F32)).astype(BF)
        fin_snd[p, 0, 64:128, :] = p_up[p, 64:128, :].astype(BF)
        first = remote(fin_snd.at[p, 0], fin_rcv.at[p, 0], f_snd.at[p, 0], f_rcv.at[p, 0], (up, e))
        first.start()
        rs_c[p][1].wait_recv()
        fin_snd[p, 1, 0:64, :] = p_dn[p, 0:64, :].astype(BF)
        fin_snd[p, 1, 64:128, :] = (p_dn[p, 64:128, :] + rs_b[p].astype(F32)).astype(BF)
        second = remote(fin_snd.at[p, 1], fin_rcv.at[p, 1], f_snd.at[p, 1], f_rcv.at[p, 1], (dn, e))
        second.start()
        fin_c[p] = (first, second)

    back_c = {}

    def stage3(p):
        fin_c[p][0].wait_recv()
        fin_c[p][1].wait_recv()
        total = p_own[p] + fin_rcv[p, 0].astype(F32) + fin_rcv[p, 1].astype(F32)
        total = total.reshape(16, 8, FQ)
        tail = jnp.concatenate([total[:, :, RET:FQ], jnp.zeros((16, 8, 2 * RET - FQ), F32)], axis=2)
        rt_snd[16 * p:16 * p + 16] = jnp.concatenate([total[:, :, 0:RET], tail], axis=1).astype(BF)
        if p == 0:
            pltpu.make_async_copy(rt_snd.at[0], rt_rcv.at[0], loc_sem.at[1]).start()
        for o in range(max(1, 16 * p), 16 * p + 16):
            back_c[o] = remote(rt_snd.at[o], rt_rcv.at[o], b_snd.at[p], b_rcv.at[p], (d, peer(BACK[o])))
            back_c[o].start()

    pair_c = []
    partner = (d, e + 1 - 2 * c0)

    def weight_grads(q):
        xq = rows[:, q, 0:64, :].reshape(n_rows, FQ)
        gu_mine[q * FQ:(q + 1) * FQ, :] = dot(xq, dgu[...], TN).astype(BF)
        part = pl.ds(q * FQ, FQ)
        c = remote(gu_mine.at[part], gu_theirs.at[part], g_snd.at[q, 0], g_rcv.at[q, 0], partner)
        c.start()
        pair_c.append(c)
        yq = rows[:, q, 64:128, :].reshape(n_rows, FQ)
        gd_mine[q] = dot(sh[...], yq, TN).astype(BF)
        c = remote(gd_mine.at[q], gd_theirs.at[q], g_snd.at[q, 1], g_rcv.at[q, 1], partner)
        c.start()
        pair_c.append(c)

    out_c = []

    def merge(q):
        replica = flag_ref[...] == 1
        part = pl.ds(q * FQ, FQ)
        pair_c[2 * q].wait_recv()
        mine = gu_mine[q * FQ:(q + 1) * FQ, :].astype(F32)
        theirs = gu_theirs[q * FQ:(q + 1) * FQ, :].astype(F32)
        gu_theirs[q * FQ:(q + 1) * FQ, :] = (mine + jnp.where(replica, theirs, 0.0)).astype(BF)
        pair_c[2 * q + 1].wait_recv()
        mine = gd_mine[q].astype(F32)
        theirs = gd_theirs[q].astype(F32)
        gd_theirs[q] = (mine + jnp.where(replica, theirs, 0.0)).astype(BF)
        copies = (
            pltpu.make_async_copy(gu_theirs.at[part, pl.ds(0, HQ)], og_ref.at[0, part], o_sem.at[q, 0]),
            pltpu.make_async_copy(gu_theirs.at[part, pl.ds(HQ, HQ)], ou_ref.at[0, part], o_sem.at[q, 1]),
            pltpu.make_async_copy(gd_theirs.at[q], od_ref.at[0, :, part], o_sem.at[q, 2]),
        )
        for c in copies:
            c.start()
        out_c.extend(copies)

    forward(0)
    for k in range(1, NCH):
        forward(k)
        relay(k - 1)
        if k == 1:
            for c in weights_in:
                c.wait()
        if k >= 3 and k % 2 == 1:
            p = (k - 3) // 2
            compute(p)
            if p >= 1:
                stage2(p - 1)
            if p >= 2:
                stage3(p - 2)
    relay(NCH - 1)
    compute(3)
    stage2(2)
    stage3(1)
    weight_grads(0)
    stage2(3)
    stage3(2)
    weight_grads(1)
    stage3(3)
    weight_grads(2)
    weight_grads(3)
    for q in range(DP):
        merge(q)

    own_back = pltpu.make_async_copy(rt_snd.at[0], rt_rcv.at[0], loc_sem.at[1])
    own_back.wait()
    for p in range(NPAIR):
        chunk_wait(rt_rcv, p, b_rcv, 16)
    copies = (
        pltpu.make_async_copy(rt_rcv, ret_ref, loc_sem.at[2]),
        pltpu.make_async_copy(sel, sel_ref, loc_sem.at[3]),
    )
    for c in copies:
        c.start()
    for k in range(NCH):
        chunk_wait(msg, k, a_snd)
        for c in (to_up[k], to_dn[k], rel_up[k], rel_dn[k]):
            c.wait_send()
    for p in range(NPAIR):
        chunk_wait(rt_snd, p, b_snd, 16)
        for c in rs_c[p] + fin_c[p]:
            c.wait_send()
    for c in pair_c:
        c.wait_send()
    for c in out_c:
        c.wait()
    for c in copies:
        c.wait()


def on_device(tokens, grad_out, routes, gates, replicated, w_gate, w_up, w_down):
    vmem = pl.BlockSpec(memory_space=pltpu.VMEM)
    hbm = pl.BlockSpec(memory_space=pl.ANY)
    dma = pltpu.SemaphoreType.DMA
    n_rows = SLOTS * CAP
    ret, sel, grad_gate, grad_up, grad_down = pl.pallas_call(
        kernel,
        out_shape=(
            jax.ShapeDtypeStruct((SLOTS, 16, RET), BF),
            jax.ShapeDtypeStruct((n_rows, TOK), BF),
            jax.ShapeDtypeStruct((1, D, HQ), BF),
            jax.ShapeDtypeStruct((1, D, HQ), BF),
            jax.ShapeDtypeStruct((1, HQ, D), BF),
        ),
        in_specs=[vmem] * 5 + [hbm] * 3,
        out_specs=(hbm,) * 5,
        scratch_shapes=[
            pltpu.VMEM((D, 2 * HQ), BF),
            pltpu.VMEM((HQ, D), BF),
            pltpu.VMEM((n_rows, TOK), BF),
            pltpu.VMEM((SLOTS, 16, MSG), BF),
            pltpu.VMEM((SLOTS, 16, MSG), BF),
            pltpu.VMEM((NCH, DP, 128, FQ), BF),
            pltpu.VMEM((n_rows, 128), F32),
            pltpu.VMEM((n_rows, 2 * HQ), BF),
            pltpu.VMEM((n_rows, HQ), BF),
            pltpu.VMEM((NPAIR, 128, FQ), BF),
            pltpu.VMEM((NPAIR, 64, FQ), BF),
            pltpu.VMEM((NPAIR, 64, FQ), BF),
            pltpu.VMEM((NPAIR, 128, FQ), F32),
            pltpu.VMEM((NPAIR, 128, FQ), F32),
            pltpu.VMEM((NPAIR, 128, FQ), F32),
            pltpu.VMEM((NPAIR, 2, 128, FQ), BF),
            pltpu.VMEM((NPAIR, 2, 128, FQ), BF),
            pltpu.VMEM((SLOTS, 16, RET), BF),
            pltpu.VMEM((SLOTS, 16, RET), BF),
            pltpu.VMEM((D, 2 * HQ), BF),
            pltpu.VMEM((DP, HQ, FQ), BF),
            pltpu.VMEM((D, 2 * HQ), BF),
            pltpu.VMEM((DP, HQ, FQ), BF),
            dma((3,)), dma((4,)),
            dma((NCH,)), dma((NCH,)),
            dma((NCH, 2)), dma((NCH, 2)),
            dma((NCH, 2)), dma((NCH, 2)),
            dma((NPAIR, 2)), dma((NPAIR, 2)),
            dma((NPAIR, 2)), dma((NPAIR, 2)),
            dma((NPAIR,)), dma((NPAIR,)),
            dma((DP, 2)), dma((DP, 2)),
            dma((DP, 3)),
        ],
        compiler_params=pltpu.CompilerParams(
            collective_id=0, has_side_effects=True, vmem_limit_bytes=60 * 2**20
        ),
        cost_estimate=pl.CostEstimate(flops=8 * 10**9, bytes_accessed=12 * 10**6, transcendentals=0),
    )(
        tokens, grad_out, routes.T, gates.astype(F32).T, replicated.reshape(1, 1),
        w_gate, w_up, w_down,
    )
    picks = sel.reshape(SLOTS, CAP, TOK)
    back = ret.reshape(SLOTS, 2, CAP, RET)
    grad_tokens = jnp.einsum("sjt,shjf->thf", picks, back, preferred_element_type=F32)
    grad_tokens = grad_tokens.reshape(TOK, 2 * RET)[:, :FQ].astype(BF)
    return grad_tokens, grad_gate, grad_up, grad_down


def solution(mesh):
    return jax.shard_map(
        on_device,
        mesh=mesh,
        in_specs=(
            P("expert", "dp"),
            P("expert", "dp"),
            P("expert", None),
            P("expert", None),
            P("expert"),
            P("expert", None, "dp"),
            P("expert", None, "dp"),
            P("expert", "dp", None),
        ),
        out_specs=(
            P("expert", "dp"),
            P("expert", None, "dp"),
            P("expert", None, "dp"),
            P("expert", "dp", None),
        ),
        check_vma=False,
    )
```

time: 396 us -> 141 us (0.36); the launches traced: 392 us -> 141 us
  waiting for transfers between devices: 230 us -> 0 us
  Pallas kernels: 0 us -> 130 us
  starting transfers between devices: 44 us -> 0 us
  blocking collectives: 27.4 us -> 0 us
  matrix products: 27.8 us -> 1.77 us
  local copies, waits for them, and re-layouts: 32.2 us -> 6.26 us
  other arithmetic: 15.3 us -> 1.22 us
  between operations: 15.1 us -> 1.31 us
    all_to_all x4 -> x0, waiting for transfers between devices: 168 us -> none  [the longest x1 77.7 us: on_device(): lax.all_to_all(packed(full_dy), 'expert', split_axis=0, concat_axis=0, ti...]
    pallas_call x0 -> x1, Pallas kernels: none -> 130 us  [on_device(): pl.pallas_call(kernel, out_shape=(jax.ShapeDtypeStruct((SLOTS, 16, RET),...]
    reduce_scatter x1 -> x0, waiting for transfers between devices: 62.2 us -> none  [on_device(): reduced = lax.psum_scatter(d_rows, 'dp', scatter_dimension=1, tiled=True)]
    all_to_all x4 -> x0, starting transfers between devices: 42.4 us -> none  [the longest x1 13 us: on_device(): lax.all_to_all(gate_buffer, 'expert', split_axis=0, concat_axis=0, tiled=...]
    all_gather x2 -> x0, blocking collectives: 27.4 us -> none  [the longest x1 13.7 us: on_device(): lax.all_gather(grad_out, 'dp', axis=1, tiled=True)]
    dot_general x8 -> x1, matrix products: 27.8 us -> 1.77 us  [on_device(): jnp.einsum('sjt,shjf->thf', picks, back, preferred_element_type=F32)]
    scatter x3 -> x0, local copies, waits for them, and re-layouts: 24 us -> none  [the longest x2 21.8 us: packed(): return jnp.zeros((buffer_rows, matrix.shape[1]), matrix.dtype).at[target]...]
    broadcast_in_dim x3 -> x0, other arithmetic: 10.8 us -> none  [on_device(): merged.append(jnp.where(replica_flag, added, mine)[None])]
  transfers between devices with their start and end apart: 8 -> 0, of which waited for: 4 -> 0; matrix products, arithmetic and copies ran while one was open for 13% -> 0% of each run, Pallas kernels for 0% -> 0%
where the time goes in v1:
time: 141 us
  Pallas kernels  130 us (92%)
  local copies, waits for them, and re-layouts  6.26 us (4%)
  matrix products  1.77 us (1%)
    pallas_call x1, Pallas kernels, on_device(): pl.pallas_call(kernel, out_shape=(jax.ShapeDtypeStruct((SLOTS, 16, RET),...  130 us
    unnamed x9, local copies, waits for them, and re-layouts  5.55 us

profile of v1, /device:TPU:1, one launch (start us, length us, event | category | flops | bytes accessed | tf_op | source)
XLA Modules:
  0.0 140.7 jit_solution(14863196724368776707)
XLA Ops:
  1.3 1.2 convert_bitcast_fusion.gates_ref
  2.5 130.1 %shard_map.111 = (bf16[64,16,512]{2,1,0:T(8,128)(2,1)}, bf16[512,128]{1,0:T(8,128)(2,1)}, bf16[1,3584,256]{2,1,0:T(8,128)(2,1)}, bf16[1,3584,256]{2,1,0:T(8,128)(2,1)}, bf16[1,256,3584]{2,1,0:T(8,128)(2,1)}) custom-call(bf16[128,896]{1,0:T(8,128)(2,1)} %tok_ref.1, bf16[128,896]{1,0:T(8,128)(2,1)} %dy_ref.1, s32[2,128]{1,0:T(2,128)} %bitcast.17, ...), custom_call_target="tpu_custom_call" | custom-call | flops 8000000000 | bytes 12000000 | tf_op jit(solution)/shard_map/pallas_call | solution.py:312
  132.7 0.0 copy-start.2
  132.7 1.8 %convolution_bitcast_fusion = bf16[128,1024]{1,0:T(8,128)(2,1)S(1)} fusion(bf16[1024,8,64]{0,1,2:T(8,128)(2,1)} %bitcast.16, bf16[512,128]{1,0:T(8,128)(2,1)} %get-tuple-element.9), kind=kOutput, calls=%fused_computation | convolution fusion | flops 134217728 | bytes 1441792 | tf_op jit(solution)/shard_map/sjt,shjf->thf/dot_general | solution.py:367
  134.4 0.7 slice.7
  135.1 0.0 copy-done.2
  135.1 0.0 copy-start.1
  135.1 1.2 copy.20
  136.4 0.9 copy-done.1
  137.3 0.0 copy-start
  137.3 1.2 copy.21
  138.5 0.9 copy-done
  139.5 1.2 copy.22
Async XLA Ops:
  132.7 2.5 %copy-start.2 = (bf16[1,3584,256]{2,1,0:T(8,128)(2,1)S(1)}, bf16[1,3584,256]{2,1,0:T(8,128)(2,1)}, u32[]{:S(2)}) copy-start(bf16[1,3584,256]{2,1,0:T(8,128)(2,1)} %get-tuple-element.19) | copy-start | bytes 5505028
  135.1 2.2 %copy-start.1 = (bf16[1,3584,256]{2,1,0:T(8,128)(2,1)S(1)}, bf16[1,3584,256]{2,1,0:T(8,128)(2,1)}, u32[]{:S(2)}) copy-start(bf16[1,3584,256]{2,1,0:T(8,128)(2,1)} %get-tuple-element.20) | copy-start | bytes 5505028
  137.3 2.2 %copy-start = (bf16[1,256,3584]{2,1,0:T(8,128)(2,1)S(1)}, bf16[1,256,3584]{2,1,0:T(8,128)(2,1)}, u32[]{:S(2)}) copy-start(bf16[1,256,3584]{2,1,0:T(8,128)(2,1)} %get-tuple-element.21) | copy-start | bytes 5505028

commit v2 on v1

--- a/solution.py
+++ b/solution.py
@@ -13,17 +13,22 @@
 FQ, HQ = D // DP, H // DP
 TOK, CAP, SLOTS = 128, 8, 64
 NX, NZ = 4, 8
+VLIM = 50 * 2**20
 NCH = 8
 NPAIR = 4
+NEAR = 3
+FAR = NCH - NEAR
 MSG = FQ + 128
+FULL = D + 128
 RET = 512
 
 
-def z_step(j):
-    return ((j + 1) // 2) * (1 if j % 2 else -1)
-
-
-OFFSETS = [(dx, z_step(j) % NZ, dc) for dx in (0, 1, 3, 2) for j in range(NZ) for dc in (0, 1)]
+LANES = [(dx, dc) for dx in range(NX) for dc in (0, 1)]
+FAR_Z = (2, -2, 3, -3, 4)
+NEAR_Z = ((1, -1), (-1, 1), (0, 0))
+OFFSETS = [(dx, FAR_Z[(k + m) % 5] % NZ, dc) for k in range(FAR) for m, (dx, dc) in enumerate(LANES)]
+OFFSETS += [(dx, dz[m % 2] % NZ, dc) for dz in NEAR_Z for m, (dx, dc) in enumerate(LANES)]
+OWN = OFFSETS.index((0, 0, 0))
 BACK = [OFFSETS.index(((-dx) % NX, (-dz) % NZ, dc)) for dx, dz, dc in OFFSETS]
 
 
@@ -36,12 +41,12 @@
 
 def kernel(
     tok_ref, dy_ref, routes_ref, gates_ref, flag_ref, wg_ref, wu_ref, wd_ref,
-    ret_ref, sel_ref, og_ref, ou_ref, od_ref,
-    wgu, wdn, sel, msg, land, rows, gcol, dgu, sh,
-    rs_snd, rs_a, rs_b, p_up, p_dn, p_own, fin_snd, fin_rcv, rt_snd, rt_rcv,
+    rt_rcv, sel, gu_sum, gd_sum,
+    wgu, wdn, full, msg, land, near_msg, near_land, rows, gcol, dgu, sh,
+    rs_snd, rs_a, rs_b, p_up, p_dn, p_own, fin_snd, fin_rcv, rt_snd,
     gu_mine, gd_mine, gu_theirs, gd_theirs,
     w_sem, loc_sem, a_snd, a_rcv, y_snd, y_rcv, r_snd, r_rcv, q_snd, q_rcv, f_snd, f_rcv,
-    b_snd, b_rcv, g_snd, g_rcv, o_sem,
+    b_snd, b_rcv, g_snd, g_rcv, t_snd, t_rcv, u_snd, u_rcv,
 ):
     d = lax.axis_index("dp")
     e = lax.axis_index("expert")
@@ -64,18 +69,17 @@
         c.start()
 
     barrier = pltpu.get_barrier_semaphore()
-    for o in range(1, SLOTS):
+    for o in range(SLOTS):
+        if o == OWN:
+            continue
         pl.semaphore_signal(barrier, inc=1, device_id=(d, peer(o)), device_id_type=MESH)
     for q in range(1, DP):
         pl.semaphore_signal(barrier, inc=1, device_id=((d + q) % DP, e), device_id_type=MESH)
 
     io = lax.broadcasted_iota(jnp.int32, (SLOTS, TOK), 0)
-    dxi = io >> 4
-    j = (io >> 1) & 7
-    mag = (j + 1) >> 1
-    slot_x = (x0 + (dxi ^ (dxi >> 1))) & (NX - 1)
-    slot_z = (z0 + jnp.where((j & 1) == 1, mag, -mag)) & (NZ - 1)
-    slot = (slot_x * NZ + slot_z) * 2 + (c0 ^ (io & 1))
+    slot = jnp.zeros((SLOTS, TOK), jnp.int32)
+    for o in range(SLOTS):
+        slot = jnp.where(io == o, peer(o), slot)
     on0 = routes_ref[0:1, :] == slot
     on1 = routes_ref[1:2, :] == slot
     hot0 = on0.astype(F32)
@@ -94,45 +98,104 @@
     sel0 = (dot(spread, rank0, NN) == place).astype(F32)
     sel1 = (dot(spread, rank1, NN) == place).astype(F32)
     sel[...] = (sel0 + sel1).astype(BF)
-    gate_of = (sel0 * gates_ref[0:1, :] + sel1 * gates_ref[1:2, :]).astype(BF)
+    gates = gates_ref[...].astype(F32)
+    gate_of = (sel0 * gates[0:1, :] + sel1 * gates[1:2, :]).astype(BF)
     gcol[...] = dot(gate_of, jnp.ones((TOK, 128), BF), NN)
 
-    a2a = {}
-    for k in range(NCH):
+    pl.semaphore_wait(barrier, SLOTS - 1 + DP - 1)
+
+    src_up = [
+        remote(tok_ref, full.at[d, 0], t_snd.at[0], t_rcv.at[0], (up, e)),
+        remote(dy_ref, full.at[d, 1], t_snd.at[1], t_rcv.at[1], (up, e)),
+    ]
+    src_dn = [
+        remote(dy_ref, full.at[d, 1], t_snd.at[2], t_rcv.at[2], (dn, e)),
+        remote(tok_ref, full.at[d, 0], t_snd.at[3], t_rcv.at[3], (dn, e)),
+    ]
+    for i in range(2):
+        src_up[i].start()
+        src_dn[i].start()
+
+    def pack(k, out, at, lane, xs, ys):
         s = sel[k * 64:(k + 1) * 64, :]
-        xk = dot(s, tok_ref[...], NN).reshape(8, 8, FQ)
-        yk = dot(s, dy_ref[...], NN).reshape(8, 8, FQ)
+        xk = dot(s, xs, NN).reshape(8, 8, FQ)
+        yk = dot(s, ys, NN).reshape(8, 8, FQ)
+        lanes = pl.ds(lane, FQ) if isinstance(lane, int) else pl.ds(pl.multiple_of(lane, 128), FQ)
+        out[at:at + 8, :, lanes] = jnp.concatenate([xk, yk], axis=1).astype(BF)
+
+    def pack_gates(k, out, at, lane):
         gk = gcol[k * 64:(k + 1) * 64, :].reshape(8, 8, 128)
-        msg[k * 8:(k + 1) * 8, :, 0:FQ] = jnp.concatenate([xk, yk], axis=1).astype(BF)
-        msg[k * 8:(k + 1) * 8, :, FQ:MSG] = jnp.concatenate([gk, gk], axis=1).astype(BF)
-        if k == 0:
-            pl.semaphore_wait(barrier, SLOTS - 1 + DP - 1)
-            own = pltpu.make_async_copy(msg.at[0], land.at[0], loc_sem.at[0])
-            own.start()
-        for o in range(max(1, 8 * k), 8 * k + 8):
-            a2a[o] = remote(msg.at[o], land.at[o], a_snd.at[k], a_rcv.at[k], (d, peer(o)))
-            a2a[o].start()
-
-    def chunk_wait(buf, k, sem, per=8):
-        lo = max(1, per * k)
-        block = buf.at[pl.ds(lo, per * k + per - lo)]
+        out[at:at + 8, :, lane:lane + 128] = jnp.concatenate([gk, gk], axis=1).astype(BF)
+
+    def send(k, src, dst, base):
+        for o in range(8 * k, 8 * k + 8):
+            if o == OWN:
+                pltpu.make_async_copy(src.at[o - base], dst.at[o - base], loc_sem.at[0]).start()
+                continue
+            remote(src.at[o - base], dst.at[o - base], a_snd.at[k], a_rcv.at[k], (d, peer(o))).start()
+
+    for k in range(FAR):
+        pack(k, msg, 8 * k, 0, tok_ref[...], dy_ref[...])
+        pack_gates(k, msg, 8 * k, FQ)
+        send(k, msg, land, 0)
+
+    def relay_source():
+        src_up[0].wait_recv()
+        part = full.at[dn, 0]
+        src_up.append(remote(part, part, u_snd.at[0], u_rcv.at[0], (up, e)))
+        src_up[2].start()
+        src_dn[0].wait_recv()
+        part = full.at[up, 1]
+        src_dn.append(remote(part, part, u_snd.at[1], u_rcv.at[1], (dn, e)))
+        src_dn[2].start()
+
+    def send_near():
+        for c in (src_up[1], src_dn[1], src_up[2], src_dn[2]):
+            c.wait_recv()
+        full[d, 0] = tok_ref[...]
+        full[d, 1] = dy_ref[...]
+        for k in range(FAR, NCH):
+            at = 8 * (k - FAR)
+            for q in range(DP):
+                pack(k, near_msg, at, q * FQ, full[q, 0], full[q, 1])
+            pack_gates(k, near_msg, at, D)
+            send(k, near_msg, near_land, 8 * FAR)
+
+    def chunk_wait(buf, k, sem, per=8, base=0):
+        lo, n = per * k, per
+        if lo <= OWN < lo + per:
+            n = per - 1
+        block = buf.at[pl.ds(lo - base, n)]
         pltpu.make_async_copy(block, block, sem.at[k]).wait()
 
     to_up, to_dn, rel_up, rel_dn = {}, {}, {}, {}
 
+    def unpack(k, block, lane, q):
+        rows[k, q, 0:64, :] = block[:, 0:8, lane:lane + FQ].reshape(64, FQ).astype(BF)
+        rows[k, q, 64:128, :] = block[:, 8:16, lane:lane + FQ].reshape(64, FQ).astype(BF)
+
     def forward(k):
-        if k == 0:
-            own.wait()
         chunk_wait(land, k, a_rcv)
         block = land[k * 8:(k + 1) * 8].astype(F32)
-        rows[k, d, 0:64, :] = block[:, 0:8, 0:FQ].reshape(64, FQ).astype(BF)
-        rows[k, d, 64:128, :] = block[:, 8:16, 0:FQ].reshape(64, FQ).astype(BF)
+        unpack(k, block, 0, d)
         gcol[k * 64:(k + 1) * 64, :] = block[:, 0:8, FQ:MSG].reshape(64, 128)
         mine = rows.at[k, d]
         to_up[k] = remote(mine, mine, y_snd.at[k, 0], y_rcv.at[k, 0], (up, e))
         to_dn[k] = remote(mine, mine, y_snd.at[k, 1], y_rcv.at[k, 1], (dn, e))
         to_up[k].start()
         to_dn[k].start()
+
+    def take_near(k):
+        if 8 * k <= OWN < 8 * k + 8:
+            at = OWN - 8 * FAR
+            pltpu.make_async_copy(near_msg.at[at], near_land.at[at], loc_sem.at[0]).wait()
+        chunk_wait(near_land, k, a_rcv, 8, 8 * FAR)
+        at = 8 * (k - FAR)
+        for q in range(DP):
+            block = near_land[at:at + 8, :, q * FQ:(q + 1) * FQ].astype(F32)
+            unpack(k, block, 0, q)
+        block = near_land[at:at + 8, :, D:FULL].astype(F32)
+        gcol[k * 64:(k + 1) * 64, :] = block[:, 0:8, :].reshape(64, 128)
 
     def relay(k):
         to_up[k].wait_recv()
@@ -152,8 +215,11 @@
 
     def compute(p):
         for k in (2 * p, 2 * p + 1):
-            rel_up[k].wait_recv()
-            rel_dn[k].wait_recv()
+            if k < FAR:
+                rel_up[k].wait_recv()
+                rel_dn[k].wait_recv()
+            else:
+                take_near(k)
         pre = jnp.zeros((128, 2 * HQ), F32)
         dh = jnp.zeros((128, HQ), F32)
         for q in range(DP):
@@ -197,8 +263,6 @@
         second.start()
         fin_c[p] = (first, second)
 
-    back_c = {}
-
     def stage3(p):
         fin_c[p][0].wait_recv()
         fin_c[p][1].wait_recv()
@@ -206,11 +270,11 @@
         total = total.reshape(16, 8, FQ)
         tail = jnp.concatenate([total[:, :, RET:FQ], jnp.zeros((16, 8, 2 * RET - FQ), F32)], axis=2)
         rt_snd[16 * p:16 * p + 16] = jnp.concatenate([total[:, :, 0:RET], tail], axis=1).astype(BF)
-        if p == 0:
-            pltpu.make_async_copy(rt_snd.at[0], rt_rcv.at[0], loc_sem.at[1]).start()
-        for o in range(max(1, 16 * p), 16 * p + 16):
-            back_c[o] = remote(rt_snd.at[o], rt_rcv.at[o], b_snd.at[p], b_rcv.at[p], (d, peer(BACK[o])))
-            back_c[o].start()
+        for o in range(16 * p, 16 * p + 16):
+            if o == OWN:
+                pltpu.make_async_copy(rt_snd.at[o], rt_rcv.at[o], loc_sem.at[1]).start()
+                continue
+            remote(rt_snd.at[o], rt_rcv.at[o], b_snd.at[p], b_rcv.at[p], (d, peer(BACK[o]))).start()
 
     pair_c = []
     partner = (d, e + 1 - 2 * c0)
@@ -228,49 +292,43 @@
         c.start()
         pair_c.append(c)
 
-    out_c = []
-
     def merge(q):
         replica = flag_ref[...] == 1
-        part = pl.ds(q * FQ, FQ)
         pair_c[2 * q].wait_recv()
         mine = gu_mine[q * FQ:(q + 1) * FQ, :].astype(F32)
         theirs = gu_theirs[q * FQ:(q + 1) * FQ, :].astype(F32)
-        gu_theirs[q * FQ:(q + 1) * FQ, :] = (mine + jnp.where(replica, theirs, 0.0)).astype(BF)
+        gu_sum[q * FQ:(q + 1) * FQ, :] = (mine + jnp.where(replica, theirs, 0.0)).astype(BF)
         pair_c[2 * q + 1].wait_recv()
         mine = gd_mine[q].astype(F32)
         theirs = gd_theirs[q].astype(F32)
-        gd_theirs[q] = (mine + jnp.where(replica, theirs, 0.0)).astype(BF)
-        copies = (
-            pltpu.make_async_copy(gu_theirs.at[part, pl.ds(0, HQ)], og_ref.at[0, part], o_sem.at[q, 0]),
-            pltpu.make_async_copy(gu_theirs.at[part, pl.ds(HQ, HQ)], ou_ref.at[0, part], o_sem.at[q, 1]),
-            pltpu.make_async_copy(gd_theirs.at[q], od_ref.at[0, :, part], o_sem.at[q, 2]),
-        )
-        for c in copies:
-            c.start()
-        out_c.extend(copies)
-
+        gd_sum[q] = (mine + jnp.where(replica, theirs, 0.0)).astype(BF)
+
+    relay_source()
     forward(0)
-    for k in range(1, NCH):
-        forward(k)
-        relay(k - 1)
-        if k == 1:
-            for c in weights_in:
-                c.wait()
-        if k >= 3 and k % 2 == 1:
-            p = (k - 3) // 2
-            compute(p)
-            if p >= 1:
-                stage2(p - 1)
-            if p >= 2:
-                stage3(p - 2)
-    relay(NCH - 1)
+    send_near()
+    forward(1)
+    relay(0)
+    forward(2)
+    relay(1)
+    for c in weights_in:
+        c.wait()
+    forward(3)
+    relay(2)
+    compute(0)
+    forward(4)
+    relay(3)
+    stage2(0)
+    relay(4)
+    compute(1)
+    stage3(0)
+    stage2(1)
+    compute(2)
+    stage3(1)
+    stage2(2)
     compute(3)
-    stage2(2)
-    stage3(1)
+    stage3(2)
     weight_grads(0)
     stage2(3)
-    stage3(2)
     weight_grads(1)
     stage3(3)
     weight_grads(2)
@@ -278,28 +336,41 @@
     for q in range(DP):
         merge(q)
 
-    own_back = pltpu.make_async_copy(rt_snd.at[0], rt_rcv.at[0], loc_sem.at[1])
-    own_back.wait()
+    pltpu.make_async_copy(rt_snd.at[OWN], rt_rcv.at[OWN], loc_sem.at[1]).wait()
     for p in range(NPAIR):
         chunk_wait(rt_rcv, p, b_rcv, 16)
-    copies = (
-        pltpu.make_async_copy(rt_rcv, ret_ref, loc_sem.at[2]),
-        pltpu.make_async_copy(sel, sel_ref, loc_sem.at[3]),
-    )
-    for c in copies:
-        c.start()
-    for k in range(NCH):
+    for k in range(FAR):
         chunk_wait(msg, k, a_snd)
         for c in (to_up[k], to_dn[k], rel_up[k], rel_dn[k]):
             c.wait_send()
+    for k in range(FAR, NCH):
+        chunk_wait(near_msg, k, a_snd, 8, 8 * FAR)
+    for c in src_up + src_dn:
+        c.wait_send()
     for p in range(NPAIR):
         chunk_wait(rt_snd, p, b_snd, 16)
         for c in rs_c[p] + fin_c[p]:
             c.wait_send()
     for c in pair_c:
         c.wait_send()
-    for c in out_c:
-        c.wait()
+
+
+def finish(ret_ref, sel_ref, gu_ref, gd_ref, gt_ref, og_ref, ou_ref, od_ref, sem):
+    copies = [
+        pltpu.make_async_copy(gu_ref.at[:, pl.ds(0, HQ)], og_ref.at[0], sem.at[0]),
+        pltpu.make_async_copy(gu_ref.at[:, pl.ds(HQ, HQ)], ou_ref.at[0], sem.at[1]),
+    ]
+    for q in range(DP):
+        copies.append(pltpu.make_async_copy(gd_ref.at[q], od_ref.at[0, :, pl.ds(q * FQ, FQ)], sem.at[2 + q]))
+    for c in copies:
+        c.start()
+    picks = sel_ref[...].astype(F32).reshape(SLOTS, CAP, TOK)
+    none = jnp.zeros_like(picks)
+    back = ret_ref[...].reshape(SLOTS * 16, RET)
+    low = jnp.concatenate([picks, none], axis=1).reshape(SLOTS * 16, TOK).astype(BF)
+    high = jnp.concatenate([none, picks], axis=1).reshape(SLOTS * 16, TOK).astype(BF)
+    gt_ref[:, 0:RET] = dot(low, back, TN).astype(BF)
+    gt_ref[:, RET:FQ] = dot(high, back, TN)[:, 0:FQ - RET].astype(BF)
     for c in copies:
         c.wait()
 
@@ -309,23 +380,24 @@
     hbm = pl.BlockSpec(memory_space=pl.ANY)
     dma = pltpu.SemaphoreType.DMA
     n_rows = SLOTS * CAP
-    ret, sel, grad_gate, grad_up, grad_down = pl.pallas_call(
+    results = pl.pallas_call(
         kernel,
         out_shape=(
-            jax.ShapeDtypeStruct((SLOTS, 16, RET), BF),
-            jax.ShapeDtypeStruct((n_rows, TOK), BF),
-            jax.ShapeDtypeStruct((1, D, HQ), BF),
-            jax.ShapeDtypeStruct((1, D, HQ), BF),
-            jax.ShapeDtypeStruct((1, HQ, D), BF),
+            pltpu.VMEM((SLOTS, 16, RET), BF),
+            pltpu.VMEM((n_rows, TOK), BF),
+            pltpu.VMEM((D, 2 * HQ), BF),
+            pltpu.VMEM((DP, HQ, FQ), BF),
         ),
         in_specs=[vmem] * 5 + [hbm] * 3,
-        out_specs=(hbm,) * 5,
+        out_specs=(vmem,) * 4,
         scratch_shapes=[
             pltpu.VMEM((D, 2 * HQ), BF),
             pltpu.VMEM((HQ, D), BF),
-            pltpu.VMEM((n_rows, TOK), BF),
-            pltpu.VMEM((SLOTS, 16, MSG), BF),
-            pltpu.VMEM((SLOTS, 16, MSG), BF),
+            pltpu.VMEM((DP, 2, TOK, FQ), BF),
+            pltpu.VMEM((8 * FAR, 16, MSG), BF),
+            pltpu.VMEM((8 * FAR, 16, MSG), BF),
+            pltpu.VMEM((8 * NEAR, 16, FULL), BF),
+            pltpu.VMEM((8 * NEAR, 16, FULL), BF),
             pltpu.VMEM((NCH, DP, 128, FQ), BF),
             pltpu.VMEM((n_rows, 128), F32),
             pltpu.VMEM((n_rows, 2 * HQ), BF),
@@ -339,12 +411,11 @@
             pltpu.VMEM((NPAIR, 2, 128, FQ), BF),
             pltpu.VMEM((NPAIR, 2, 128, FQ), BF),
             pltpu.VMEM((SLOTS, 16, RET), BF),
-            pltpu.VMEM((SLOTS, 16, RET), BF),
             pltpu.VMEM((D, 2 * HQ), BF),
             pltpu.VMEM((DP, HQ, FQ), BF),
             pltpu.VMEM((D, 2 * HQ), BF),
             pltpu.VMEM((DP, HQ, FQ), BF),
-            dma((3,)), dma((4,)),
+            dma((3,)), dma((2,)),
             dma((NCH,)), dma((NCH,)),
             dma((NCH, 2)), dma((NCH, 2)),
             dma((NCH, 2)), dma((NCH, 2)),
@@ -352,21 +423,30 @@
             dma((NPAIR, 2)), dma((NPAIR, 2)),
             dma((NPAIR,)), dma((NPAIR,)),
             dma((DP, 2)), dma((DP, 2)),
-            dma((DP, 3)),
+            dma((4,)), dma((4,)), dma((2,)), dma((2,)),
         ],
         compiler_params=pltpu.CompilerParams(
-            collective_id=0, has_side_effects=True, vmem_limit_bytes=60 * 2**20
+            collective_id=0, has_side_effects=True, vmem_limit_bytes=VLIM
         ),
         cost_estimate=pl.CostEstimate(flops=8 * 10**9, bytes_accessed=12 * 10**6, transcendentals=0),
     )(
-        tokens, grad_out, routes.T, gates.astype(F32).T, replicated.reshape(1, 1),
+        tokens, grad_out, routes.T, gates.T, replicated.reshape(1, 1),
         w_gate, w_up, w_down,
     )
-    picks = sel.reshape(SLOTS, CAP, TOK)
-    back = ret.reshape(SLOTS, 2, CAP, RET)
-    grad_tokens = jnp.einsum("sjt,shjf->thf", picks, back, preferred_element_type=F32)
-    grad_tokens = grad_tokens.reshape(TOK, 2 * RET)[:, :FQ].astype(BF)
-    return grad_tokens, grad_gate, grad_up, grad_down
+    return pl.pallas_call(
+        finish,
+        out_shape=(
+            jax.ShapeDtypeStruct((TOK, FQ), BF),
+            jax.ShapeDtypeStruct((1, D, HQ), BF),
+            jax.ShapeDtypeStruct((1, D, HQ), BF),
+            jax.ShapeDtypeStruct((1, HQ, D), BF),
+        ),
+        in_specs=[vmem] * 4,
+        out_specs=(vmem,) + (hbm,) * 3,
+        scratch_shapes=[dma((2 + DP,))],
+        compiler_params=pltpu.CompilerParams(vmem_limit_bytes=16 * 2**20),
+        cost_estimate=pl.CostEstimate(flops=3 * 10**8, bytes_accessed=7 * 10**6, transcendentals=0),
+    )(*results)
 
 
 def solution(mesh):

time: 141 us -> 116 us (0.82)
  Pallas kernels: 130 us -> 114 us
  local copies, waits for them, and re-layouts: 6.26 us -> 0 us
  matrix products: 1.77 us -> 0 us
    pallas_call x1 -> x2, Pallas kernels: 130 us -> 114 us  [the longest x1 111 us: on_device(): pl.pallas_call(kernel, out_shape=(pltpu.VMEM((SLOTS, 16, RET), BF), pltpu...]
    unnamed x9 -> x0, local copies, waits for them, and re-layouts: 5.55 us -> none
    dot_general x1 -> x0, matrix products: 1.77 us -> none  [on_device(): jnp.einsum('sjt,shjf->thf', picks, back, preferred_element_type=F32)]
where the time goes in v2:
time: 116 us
  Pallas kernels  114 us (98%)
  between operations  1.47 us (1%)
    pallas_call x1, Pallas kernels, on_device(): pl.pallas_call(kernel, out_shape=(pltpu.VMEM((SLOTS, 16, RET), BF), pltpu...  111 us
    pallas_call x1, Pallas kernels, on_device(): pl.pallas_call(finish, out_shape=(jax.ShapeDtypeStruct((TOK, FQ), BF), ja...  3.28 us

profile of v2, /device:TPU:1, one launch (start us, length us, event | category | flops | bytes accessed | tf_op | source)
XLA Modules:
  0.0 115.8 jit_solution(10612915611964381971)
XLA Ops:
  1.3 111.1 %shard_map.111 = (bf16[64,16,512]{2,1,0:T(8,128)(2,1)S(1)}, bf16[512,128]{1,0:T(8,128)(2,1)S(1)}, bf16[3584,512]{1,0:T(8,128)(2,1)S(1)}, bf16[4,256,896]{2,1,0:T(8,128)(2,1)S(1)}) custom-call(bf16[128,896]{1,0:T(8,128)(2,1)} %tok_ref.1, bf16[128,896]{1,0:T(8,128)(2,1)} %dy_ref.1, s32[2,128]{1,0:T(2,128)} %bitcast.4, bf16[2,128]{1,0:T(2,128)(2,1)} %bitcast.5, ...), custom_call_target="tpu_custom_call" | custom-call | flops 8000000000 | bytes 12000000 | tf_op jit(solution)/shard_map/pallas_call | solution.py:383
  112.3 3.3 %shard_map.112 = (bf16[128,896]{1,0:T(8,128)(2,1)}, bf16[1,3584,256]{2,1,0:T(8,128)(2,1)}, bf16[1,3584,256]{2,1,0:T(8,128)(2,1)}, bf16[1,256,3584]{2,1,0:T(8,128)(2,1)}) custom-call(bf16[64,16,512]{2,1,0:T(8,128)(2,1)S(1)} %get-tuple-element.8.ret_ref, bf16[512,128]{1,0:T(8,128)(2,1)S(1)} %get-tuple-element.9.sel_ref, ...), custom_call_target="tpu_custom_call" | custom-call | flops 300000000 | bytes 7000000 | tf_op jit(solution)/shard_map/pallas_call | solution.py:436

commit v3 on v2

--- a/solution.py
+++ b/solution.py
@@ -18,16 +18,16 @@
 NPAIR = 4
 NEAR = 3
 FAR = NCH - NEAR
-MSG = FQ + 128
-FULL = D + 128
 RET = 512
 
 
-LANES = [(dx, dc) for dx in range(NX) for dc in (0, 1)]
-FAR_Z = (2, -2, 3, -3, 4)
-NEAR_Z = ((1, -1), (-1, 1), (0, 0))
-OFFSETS = [(dx, FAR_Z[(k + m) % 5] % NZ, dc) for k in range(FAR) for m, (dx, dc) in enumerate(LANES)]
-OFFSETS += [(dx, dz[m % 2] % NZ, dc) for dz in NEAR_Z for m, (dx, dc) in enumerate(LANES)]
+NEAR_OFFSETS = [(dx, dz, dc) for dx, dz in ((0, 2), (0, -2), (1, 1), (-1, -1)) for dc in (0, 1)]
+NEAR_OFFSETS += [(dx, dz, dc) for dx, dz in ((0, 1), (0, -1), (1, -1), (-1, 1)) for dc in (0, 1)]
+NEAR_OFFSETS += [(dx, 0, dc) for dx in (0, 1, -1, 2) for dc in (0, 1)]
+NEAR_OFFSETS = [(dx % NX, dz % NZ, dc) for dx, dz, dc in NEAR_OFFSETS]
+FAR_OFFSETS = [(dx, dz, dc) for dz in range(NZ) for dx in range(NX) for dc in (0, 1)]
+FAR_OFFSETS = [o for o in FAR_OFFSETS if o not in NEAR_OFFSETS]
+OFFSETS = [o for k in range(FAR) for o in FAR_OFFSETS[k::FAR]] + NEAR_OFFSETS
 OWN = OFFSETS.index((0, 0, 0))
 BACK = [OFFSETS.index(((-dx) % NX, (-dz) % NZ, dc)) for dx, dz, dc in OFFSETS]
 
@@ -42,11 +42,11 @@
 def kernel(
     tok_ref, dy_ref, routes_ref, gates_ref, flag_ref, wg_ref, wu_ref, wd_ref,
     rt_rcv, sel, gu_sum, gd_sum,
-    wgu, wdn, full, msg, land, near_msg, near_land, rows, gcol, dgu, sh,
+    wgu, wdn, full, msg, land, near_msg, near_land, rows, g_msg, g_land, g_rows, dgu, sh,
     rs_snd, rs_a, rs_b, p_up, p_dn, p_own, fin_snd, fin_rcv, rt_snd,
     gu_mine, gd_mine, gu_theirs, gd_theirs,
     w_sem, loc_sem, a_snd, a_rcv, y_snd, y_rcv, r_snd, r_rcv, q_snd, q_rcv, f_snd, f_rcv,
-    b_snd, b_rcv, g_snd, g_rcv, t_snd, t_rcv, u_snd, u_rcv,
+    b_snd, b_rcv, g_snd, g_rcv, t_snd, t_rcv, u_snd, u_rcv, gt_snd, gt_rcv, gs_snd, gs_rcv, sync,
 ):
     d = lax.axis_index("dp")
     e = lax.axis_index("expert")
@@ -69,12 +69,15 @@
         c.start()
 
     barrier = pltpu.get_barrier_semaphore()
-    for o in range(SLOTS):
-        if o == OWN:
-            continue
-        pl.semaphore_signal(barrier, inc=1, device_id=(d, peer(o)), device_id_type=MESH)
-    for q in range(1, DP):
-        pl.semaphore_signal(barrier, inc=1, device_id=((d + q) % DP, e), device_id_type=MESH)
+    def greet(sem, devices):
+        for dev in devices:
+            pl.semaphore_signal(sem, inc=1, device_id=dev, device_id_type=MESH)
+
+    along_x = [(d, ((x0 + i) % NX * NZ + z0) * 2 + c0) for i in range(1, NX)]
+    along_z = [(d, (x0 * NZ + (z0 + i) % NZ) * 2 + c0) for i in range(1, NZ)]
+    partner = (d, e + 1 - 2 * c0)
+    along_y = [((d + i) % DP, e) for i in range(1, DP)]
+    greet(barrier, along_y + along_z + along_x + [partner])
 
     io = lax.broadcasted_iota(jnp.int32, (SLOTS, TOK), 0)
     slot = jnp.zeros((SLOTS, TOK), jnp.int32)
@@ -100,9 +103,11 @@
     sel[...] = (sel0 + sel1).astype(BF)
     gates = gates_ref[...].astype(F32)
     gate_of = (sel0 * gates[0:1, :] + sel1 * gates[1:2, :]).astype(BF)
-    gcol[...] = dot(gate_of, jnp.ones((TOK, 128), BF), NN)
-
-    pl.semaphore_wait(barrier, SLOTS - 1 + DP - 1)
+    gates_of = dot(gate_of, jnp.ones((TOK, 128), BF), NN).reshape(SLOTS, CAP, 128)
+    g_msg[...] = jnp.concatenate([gates_of, gates_of], axis=1).astype(BF)
+
+    pl.semaphore_wait(barrier, DP + NZ + NX - 3 + 1)
+    greet(sync.at[0], along_x)
 
     src_up = [
         remote(tok_ref, full.at[d, 0], t_snd.at[0], t_rcv.at[0], (up, e)),
@@ -123,10 +128,6 @@
         lanes = pl.ds(lane, FQ) if isinstance(lane, int) else pl.ds(pl.multiple_of(lane, 128), FQ)
         out[at:at + 8, :, lanes] = jnp.concatenate([xk, yk], axis=1).astype(BF)
 
-    def pack_gates(k, out, at, lane):
-        gk = gcol[k * 64:(k + 1) * 64, :].reshape(8, 8, 128)
-        out[at:at + 8, :, lane:lane + 128] = jnp.concatenate([gk, gk], axis=1).astype(BF)
-
     def send(k, src, dst, base):
         for o in range(8 * k, 8 * k + 8):
             if o == OWN:
@@ -134,9 +135,42 @@
                 continue
             remote(src.at[o - base], dst.at[o - base], a_snd.at[k], a_rcv.at[k], (d, peer(o))).start()
 
+    def each_dp(act):
+        for p in range(DP):
+            pl.when(d == p)(functools.partial(act, p))
+
+    def send_gates(p):
+        for o in range(16 * p, 16 * p + 16):
+            if o == OWN:
+                pltpu.make_async_copy(g_msg.at[o], g_land.at[o - 16 * p], loc_sem.at[2]).start()
+                continue
+            remote(g_msg.at[o], g_land.at[o - 16 * p], gt_snd.at[0], gt_rcv.at[0], (d, peer(o))).start()
+
+    def gates_wait(sem, p):
+        n = 15 if 16 * p <= OWN < 16 * p + 16 else 16
+        block = g_land.at[pl.ds(0, n)]
+        pltpu.make_async_copy(block, block, sem.at[0]).wait()
+
+    def take_gates(p):
+        if 16 * p <= OWN < 16 * p + 16:
+            pltpu.make_async_copy(g_msg.at[OWN], g_land.at[OWN - 16 * p], loc_sem.at[2]).wait()
+        gates_wait(gt_rcv, p)
+
+    def share_gates():
+        each_dp(take_gates)
+        g_rows[d] = g_land[...].astype(F32)[:, 0:8, :].reshape(128, 128).astype(BF)
+        for i, to in enumerate((up, op, dn)):
+            gate_c.append(remote(g_rows.at[d], g_rows.at[d], gs_snd.at[i], gs_rcv.at[i], (to, e)))
+            gate_c[i].start()
+
+    gate_c = []
     for k in range(FAR):
         pack(k, msg, 8 * k, 0, tok_ref[...], dy_ref[...])
-        pack_gates(k, msg, 8 * k, FQ)
+        if k == 0:
+            pl.semaphore_wait(sync.at[0], NX - 1)
+            greet(sync.at[1], [partner])
+            pl.semaphore_wait(sync.at[1], 1)
+            each_dp(send_gates)
         send(k, msg, land, 0)
 
     def relay_source():
@@ -158,7 +192,6 @@
             at = 8 * (k - FAR)
             for q in range(DP):
                 pack(k, near_msg, at, q * FQ, full[q, 0], full[q, 1])
-            pack_gates(k, near_msg, at, D)
             send(k, near_msg, near_land, 8 * FAR)
 
     def chunk_wait(buf, k, sem, per=8, base=0):
@@ -178,7 +211,6 @@
         chunk_wait(land, k, a_rcv)
         block = land[k * 8:(k + 1) * 8].astype(F32)
         unpack(k, block, 0, d)
-        gcol[k * 64:(k + 1) * 64, :] = block[:, 0:8, FQ:MSG].reshape(64, 128)
         mine = rows.at[k, d]
         to_up[k] = remote(mine, mine, y_snd.at[k, 0], y_rcv.at[k, 0], (up, e))
         to_dn[k] = remote(mine, mine, y_snd.at[k, 1], y_rcv.at[k, 1], (dn, e))
@@ -194,8 +226,6 @@
         for q in range(DP):
             block = near_land[at:at + 8, :, q * FQ:(q + 1) * FQ].astype(F32)
             unpack(k, block, 0, q)
-        block = near_land[at:at + 8, :, D:FULL].astype(F32)
-        gcol[k * 64:(k + 1) * 64, :] = block[:, 0:8, :].reshape(64, 128)
 
     def relay(k):
         to_up[k].wait_recv()
@@ -227,7 +257,7 @@
             yq = rows[2 * p:2 * p + 2, q, 64:128, :].reshape(128, FQ)
             pre = pre + dot(xq, wgu[q * FQ:(q + 1) * FQ, :], NN)
             dh = dh + dot(yq, wdn[:, q * FQ:(q + 1) * FQ], NT)
-        g = gcol[p * 128:(p + 1) * 128, :]
+        g = g_rows[p].astype(F32)
         g = jnp.concatenate([g, g], axis=1)
         pg, pu = pre[:, 0:HQ], pre[:, HQ:]
         sig = jax.nn.sigmoid(pg)
@@ -237,48 +267,47 @@
         sh[span, :] = (g * act * pu).astype(BF)
         dgu[span, 0:HQ] = (dh * pu * sig * (1.0 + pg * (1.0 - sig))).astype(BF)
         dgu[span, HQ:] = (dh * act).astype(BF)
-        rs_snd[p] = row_part(p, op).astype(BF)
-        rs_c[p] = (
-            remote(rs_snd.at[p, pl.ds(0, 64)], rs_a.at[p], q_snd.at[p, 0], q_rcv.at[p, 0], (up, e)),
-            remote(rs_snd.at[p, pl.ds(64, 64)], rs_b.at[p], q_snd.at[p, 1], q_rcv.at[p, 1], (dn, e)),
-        )
-        for c in rs_c[p]:
-            c.start()
-        p_up[p] = row_part(p, up)
-        p_dn[p] = row_part(p, dn)
-        p_own[p] = row_part(p, d)
+        rs_snd[2 * p:2 * p + 2] = row_part(p, op).astype(BF).reshape(2, 64, FQ)
+        for k in (2 * p, 2 * p + 1):
+            rs_c[k] = (
+                remote(rs_snd.at[k, pl.ds(0, 32)], rs_a.at[k], q_snd.at[k, 0], q_rcv.at[k, 0], (up, e)),
+                remote(rs_snd.at[k, pl.ds(32, 32)], rs_b.at[k], q_snd.at[k, 1], q_rcv.at[k, 1], (dn, e)),
+            )
+            for c in rs_c[k]:
+                c.start()
+        p_up[2 * p:2 * p + 2] = row_part(p, up).reshape(2, 64, FQ)
+        p_dn[2 * p:2 * p + 2] = row_part(p, dn).reshape(2, 64, FQ)
+        p_own[2 * p:2 * p + 2] = row_part(p, d).reshape(2, 64, FQ)
 
     fin_c = {}
 
-    def stage2(p):
-        rs_c[p][0].wait_recv()
-        fin_snd[p, 0, 0:64, :] = (p_up[p, 0:64, :] + rs_a[p].astype(F32)).astype(BF)
-        fin_snd[p, 0, 64:128, :] = p_up[p, 64:128, :].astype(BF)
-        first = remote(fin_snd.at[p, 0], fin_rcv.at[p, 0], f_snd.at[p, 0], f_rcv.at[p, 0], (up, e))
+    def stage2(k):
+        rs_c[k][0].wait_recv()
+        fin_snd[k, 0, 0:32, :] = (p_up[k, 0:32, :] + rs_a[k].astype(F32)).astype(BF)
+        fin_snd[k, 0, 32:64, :] = p_up[k, 32:64, :].astype(BF)
+        first = remote(fin_snd.at[k, 0], fin_rcv.at[k, 0], f_snd.at[k, 0], f_rcv.at[k, 0], (up, e))
         first.start()
-        rs_c[p][1].wait_recv()
-        fin_snd[p, 1, 0:64, :] = p_dn[p, 0:64, :].astype(BF)
-        fin_snd[p, 1, 64:128, :] = (p_dn[p, 64:128, :] + rs_b[p].astype(F32)).astype(BF)
-        second = remote(fin_snd.at[p, 1], fin_rcv.at[p, 1], f_snd.at[p, 1], f_rcv.at[p, 1], (dn, e))
+        rs_c[k][1].wait_recv()
+        fin_snd[k, 1, 0:32, :] = p_dn[k, 0:32, :].astype(BF)
+        fin_snd[k, 1, 32:64, :] = (p_dn[k, 32:64, :] + rs_b[k].astype(F32)).astype(BF)
+        second = remote(fin_snd.at[k, 1], fin_rcv.at[k, 1], f_snd.at[k, 1], f_rcv.at[k, 1], (dn, e))
         second.start()
-        fin_c[p] = (first, second)
-
-    def stage3(p):
-        fin_c[p][0].wait_recv()
-        fin_c[p][1].wait_recv()
-        total = p_own[p] + fin_rcv[p, 0].astype(F32) + fin_rcv[p, 1].astype(F32)
-        total = total.reshape(16, 8, FQ)
-        tail = jnp.concatenate([total[:, :, RET:FQ], jnp.zeros((16, 8, 2 * RET - FQ), F32)], axis=2)
-        rt_snd[16 * p:16 * p + 16] = jnp.concatenate([total[:, :, 0:RET], tail], axis=1).astype(BF)
-        for o in range(16 * p, 16 * p + 16):
+        fin_c[k] = (first, second)
+
+    def stage3(k):
+        fin_c[k][0].wait_recv()
+        fin_c[k][1].wait_recv()
+        total = p_own[k] + fin_rcv[k, 0].astype(F32) + fin_rcv[k, 1].astype(F32)
+        total = total.reshape(8, 8, FQ)
+        tail = jnp.concatenate([total[:, :, RET:FQ], jnp.zeros((8, 8, 2 * RET - FQ), F32)], axis=2)
+        rt_snd[8 * k:8 * k + 8] = jnp.concatenate([total[:, :, 0:RET], tail], axis=1).astype(BF)
+        for o in range(8 * k, 8 * k + 8):
             if o == OWN:
                 pltpu.make_async_copy(rt_snd.at[o], rt_rcv.at[o], loc_sem.at[1]).start()
                 continue
-            remote(rt_snd.at[o], rt_rcv.at[o], b_snd.at[p], b_rcv.at[p], (d, peer(BACK[o]))).start()
+            remote(rt_snd.at[o], rt_rcv.at[o], b_snd.at[k], b_rcv.at[k], (d, peer(BACK[o]))).start()
 
     pair_c = []
-    partner = (d, e + 1 - 2 * c0)
-
     def weight_grads(q):
         xq = rows[:, q, 0:64, :].reshape(n_rows, FQ)
         gu_mine[q * FQ:(q + 1) * FQ, :] = dot(xq, dgu[...], TN).astype(BF)
@@ -307,38 +336,49 @@
     forward(0)
     send_near()
     forward(1)
+    share_gates()
     relay(0)
     forward(2)
     relay(1)
     for c in weights_in:
         c.wait()
+    for c in gate_c:
+        c.wait_recv()
     forward(3)
     relay(2)
     compute(0)
     forward(4)
     relay(3)
     stage2(0)
+    stage2(1)
     relay(4)
     compute(1)
     stage3(0)
-    stage2(1)
-    compute(2)
     stage3(1)
     stage2(2)
+    stage2(3)
+    compute(2)
+    stage3(2)
+    stage3(3)
+    stage2(4)
+    stage2(5)
     compute(3)
-    stage3(2)
+    stage3(4)
+    stage3(5)
     weight_grads(0)
-    stage2(3)
+    stage2(6)
+    stage2(7)
     weight_grads(1)
-    stage3(3)
     weight_grads(2)
+    stage3(6)
     weight_grads(3)
+    stage3(7)
     for q in range(DP):
         merge(q)
 
     pltpu.make_async_copy(rt_snd.at[OWN], rt_rcv.at[OWN], loc_sem.at[1]).wait()
-    for p in range(NPAIR):
-        chunk_wait(rt_rcv, p, b_rcv, 16)
+    for k in range(NCH):
+        chunk_wait(rt_rcv, k, b_rcv)
     for k in range(FAR):
         chunk_wait(msg, k, a_snd)
         for c in (to_up[k], to_dn[k], rel_up[k], rel_dn[k]):
@@ -347,10 +387,13 @@
         chunk_wait(near_msg, k, a_snd, 8, 8 * FAR)
     for c in src_up + src_dn:
         c.wait_send()
-    for p in range(NPAIR):
-        chunk_wait(rt_snd, p, b_snd, 16)
-        for c in rs_c[p] + fin_c[p]:
+    for k in range(NCH):
+        chunk_wait(rt_snd, k, b_snd)
+        for c in rs_c[k] + fin_c[k]:
             c.wait_send()
+    for c in gate_c:
+        c.wait_send()
+    each_dp(functools.partial(gates_wait, gt_snd))
     for c in pair_c:
         c.wait_send()
 
@@ -394,36 +437,39 @@
             pltpu.VMEM((D, 2 * HQ), BF),
             pltpu.VMEM((HQ, D), BF),
             pltpu.VMEM((DP, 2, TOK, FQ), BF),
-            pltpu.VMEM((8 * FAR, 16, MSG), BF),
-            pltpu.VMEM((8 * FAR, 16, MSG), BF),
-            pltpu.VMEM((8 * NEAR, 16, FULL), BF),
-            pltpu.VMEM((8 * NEAR, 16, FULL), BF),
+            pltpu.VMEM((8 * FAR, 16, FQ), BF),
+            pltpu.VMEM((8 * FAR, 16, FQ), BF),
+            pltpu.VMEM((8 * NEAR, 16, D), BF),
+            pltpu.VMEM((8 * NEAR, 16, D), BF),
             pltpu.VMEM((NCH, DP, 128, FQ), BF),
-            pltpu.VMEM((n_rows, 128), F32),
+            pltpu.VMEM((SLOTS, 16, 128), BF),
+            pltpu.VMEM((16, 16, 128), BF),
+            pltpu.VMEM((DP, 128, 128), BF),
             pltpu.VMEM((n_rows, 2 * HQ), BF),
             pltpu.VMEM((n_rows, HQ), BF),
-            pltpu.VMEM((NPAIR, 128, FQ), BF),
-            pltpu.VMEM((NPAIR, 64, FQ), BF),
-            pltpu.VMEM((NPAIR, 64, FQ), BF),
-            pltpu.VMEM((NPAIR, 128, FQ), F32),
-            pltpu.VMEM((NPAIR, 128, FQ), F32),
-            pltpu.VMEM((NPAIR, 128, FQ), F32),
-            pltpu.VMEM((NPAIR, 2, 128, FQ), BF),
-            pltpu.VMEM((NPAIR, 2, 128, FQ), BF),
+            pltpu.VMEM((NCH, 64, FQ), BF),
+            pltpu.VMEM((NCH, 32, FQ), BF),
+            pltpu.VMEM((NCH, 32, FQ), BF),
+            pltpu.VMEM((NCH, 64, FQ), F32),
+            pltpu.VMEM((NCH, 64, FQ), F32),
+            pltpu.VMEM((NCH, 64, FQ), F32),
+            pltpu.VMEM((NCH, 2, 64, FQ), BF),
+            pltpu.VMEM((NCH, 2, 64, FQ), BF),
             pltpu.VMEM((SLOTS, 16, RET), BF),
             pltpu.VMEM((D, 2 * HQ), BF),
             pltpu.VMEM((DP, HQ, FQ), BF),
             pltpu.VMEM((D, 2 * HQ), BF),
             pltpu.VMEM((DP, HQ, FQ), BF),
-            dma((3,)), dma((2,)),
+            dma((3,)), dma((3,)),
             dma((NCH,)), dma((NCH,)),
             dma((NCH, 2)), dma((NCH, 2)),
             dma((NCH, 2)), dma((NCH, 2)),
-            dma((NPAIR, 2)), dma((NPAIR, 2)),
-            dma((NPAIR, 2)), dma((NPAIR, 2)),
-            dma((NPAIR,)), dma((NPAIR,)),
+            dma((NCH, 2)), dma((NCH, 2)),
+            dma((NCH, 2)), dma((NCH, 2)),
+            dma((NCH,)), dma((NCH,)),
             dma((DP, 2)), dma((DP, 2)),
             dma((4,)), dma((4,)), dma((2,)), dma((2,)),
+            dma((1,)), dma((1,)), dma((3,)), dma((3,)), pltpu.SemaphoreType.REGULAR((2,)),
         ],
         compiler_params=pltpu.CompilerParams(
             collective_id=0, has_side_effects=True, vmem_limit_bytes=VLIM

time: 116 us -> 110 us (0.948)
  Pallas kernels: 114 us -> 108 us
    pallas_call x1, Pallas kernels: 111 us -> 105 us  [on_device(): pl.pallas_call(kernel, out_shape=(pltpu.VMEM((SLOTS, 16, RET), BF), pltpu...]
where the time goes in v3:
time: 110 us
  Pallas kernels  108 us (98%)
  between operations  1.47 us (1%)
    pallas_call x1, Pallas kernels, on_device(): pl.pallas_call(kernel, out_shape=(pltpu.VMEM((SLOTS, 16, RET), BF), pltpu...  105 us
    pallas_call x1, Pallas kernels, on_device(): pl.pallas_call(finish, out_shape=(jax.ShapeDtypeStruct((TOK, FQ), BF), ja...  3.28 us

profile of v3, /device:TPU:1, one launch (start us, length us, event | category | flops | bytes accessed | tf_op | source)
XLA Modules:
  0.0 109.9 jit_solution(3024139863340433183)
XLA Ops:
  1.3 105.2 %shard_map.111 = (bf16[64,16,512]{2,1,0:T(8,128)(2,1)S(1)}, bf16[512,128]{1,0:T(8,128)(2,1)S(1)}, bf16[3584,512]{1,0:T(8,128)(2,1)S(1)}, bf16[4,256,896]{2,1,0:T(8,128)(2,1)S(1)}) custom-call(bf16[128,896]{1,0:T(8,128)(2,1)} %tok_ref.1, bf16[128,896]{1,0:T(8,128)(2,1)} %dy_ref.1, s32[2,128]{1,0:T(2,128)} %bitcast.4, bf16[2,128]{1,0:T(2,128)(2,1)} %bitcast.5, ...), custom_call_target="tpu_custom_call" | custom-call | flops 8000000000 | bytes 12000000 | tf_op jit(solution)/shard_map/pallas_call | solution.py:426
  106.5 3.3 %shard_map.112 = (bf16[128,896]{1,0:T(8,128)(2,1)}, bf16[1,3584,256]{2,1,0:T(8,128)(2,1)}, bf16[1,3584,256]{2,1,0:T(8,128)(2,1)}, bf16[1,256,3584]{2,1,0:T(8,128)(2,1)}) custom-call(bf16[64,16,512]{2,1,0:T(8,128)(2,1)S(1)} %get-tuple-element.8.ret_ref, bf16[512,128]{1,0:T(8,128)(2,1)S(1)} %get-tuple-element.9.sel_ref, ...), custom_call_target="tpu_custom_call" | custom-call | flops 300000000 | bytes 7000000 | tf_op jit(solution)/shard_map/pallas_call | solution.py:482

commit v4 on v3

--- a/solution.py
+++ b/solution.py
@@ -322,7 +322,7 @@
         pair_c.append(c)
 
     def merge(q):
-        replica = flag_ref[...] == 1
+        replica = flag_ref[0] == 1
         pair_c[2 * q].wait_recv()
         mine = gu_mine[q * FQ:(q + 1) * FQ, :].astype(F32)
         theirs = gu_theirs[q * FQ:(q + 1) * FQ, :].astype(F32)
@@ -370,11 +370,13 @@
     stage2(7)
     weight_grads(1)
     weight_grads(2)
+    weight_grads(3)
     stage3(6)
-    weight_grads(3)
+    merge(0)
+    merge(1)
     stage3(7)
-    for q in range(DP):
-        merge(q)
+    merge(2)
+    merge(3)
 
     pltpu.make_async_copy(rt_snd.at[OWN], rt_rcv.at[OWN], loc_sem.at[1]).wait()
     for k in range(NCH):
@@ -431,7 +433,7 @@
             pltpu.VMEM((D, 2 * HQ), BF),
             pltpu.VMEM((DP, HQ, FQ), BF),
         ),
-        in_specs=[vmem] * 5 + [hbm] * 3,
+        in_specs=[vmem] * 4 + [pl.BlockSpec(memory_space=pltpu.SMEM)] + [hbm] * 3,
         out_specs=(vmem,) * 4,
         scratch_shapes=[
             pltpu.VMEM((D, 2 * HQ), BF),
@@ -476,7 +478,7 @@
         ),
         cost_estimate=pl.CostEstimate(flops=8 * 10**9, bytes_accessed=12 * 10**6, transcendentals=0),
     )(
-        tokens, grad_out, routes.T, gates.T, replicated.reshape(1, 1),
+        tokens, grad_out, routes.T, gates.T, replicated,
         w_gate, w_up, w_down,
     )
     return pl.pallas_call(

time: 110 us -> 110 us (level)
  no operation moved by 1% of the time
where the time goes in v4:
time: 110 us
  Pallas kernels  108 us (98%)
  between operations  1.47 us (1%)
    pallas_call x1, Pallas kernels, on_device(): pl.pallas_call(kernel, out_shape=(pltpu.VMEM((SLOTS, 16, RET), BF), pltpu...  105 us
    pallas_call x1, Pallas kernels, on_device(): pl.pallas_call(finish, out_shape=(jax.ShapeDtypeStruct((TOK, FQ), BF), ja...  3.27 us

profile of v4, /device:TPU:1, one launch (start us, length us, event | category | flops | bytes accessed | tf_op | source)
XLA Modules:
  0.0 109.7 jit_solution(14951848773173883668)
XLA Ops:
  1.3 105.0 %shard_map.111 = (bf16[64,16,512]{2,1,0:T(8,128)(2,1)S(1)}, bf16[512,128]{1,0:T(8,128)(2,1)S(1)}, bf16[3584,512]{1,0:T(8,128)(2,1)S(1)}, bf16[4,256,896]{2,1,0:T(8,128)(2,1)S(1)}) custom-call(bf16[128,896]{1,0:T(8,128)(2,1)} %tok_ref.1, bf16[128,896]{1,0:T(8,128)(2,1)} %dy_ref.1, s32[2,128]{1,0:T(2,128)} %bitcast.2, bf16[2,128]{1,0:T(2,128)(2,1)} %bitcast.3, ...), custom_call_target="tpu_custom_call" | custom-call | flops 8000000000 | bytes 12000000 | tf_op jit(solution)/shard_map/pallas_call | solution.py:428
  106.3 3.3 %shard_map.112 = (bf16[128,896]{1,0:T(8,128)(2,1)}, bf16[1,3584,256]{2,1,0:T(8,128)(2,1)}, bf16[1,3584,256]{2,1,0:T(8,128)(2,1)}, bf16[1,256,3584]{2,1,0:T(8,128)(2,1)}) custom-call(bf16[64,16,512]{2,1,0:T(8,128)(2,1)S(1)} %get-tuple-element.8.ret_ref, bf16[512,128]{1,0:T(8,128)(2,1)S(1)} %get-tuple-element.9.sel_ref, ...), custom_call_target="tpu_custom_call" | custom-call | flops 300000000 | bytes 7000000 | tf_op jit(solution)/shard_map/pallas_call | solution.py:484
